TPU v7x, 32 devices: a whole 2x2x4 slice. The times are simulated.
32 devices in a mesh: grp: 2 (over x), tok: 8 (over z, y), sub: 2 (over core).
Axes of the slice: x: 2, y: 2, z: 4, core: 2. Of those that a mesh axis runs over, the one named last changes fastest.
Arguments:
- patches: bfloat16 [4096, 1408], P(('grp', 'tok')), may hold values from -6 to 6
- image_sizes: int32 [16, 4], P(('grp', 'tok')), may hold values from 1 to 32, 64 in all within a row
- vision_inproj: bfloat16 [1408, 2, 3, 704], P('tok', 'sub'), may hold values from -0.15625 to 0.15625
- vision_outproj: bfloat16 [1408, 1408], P('sub', 'tok'), may hold values from -0.625 to 0.625
- merger_weight: bfloat16 [5632, 1408], P('tok', 'sub'), may hold values from -0.078125 to 0.078125
- text_embed: bfloat16 [2048, 1408], P(('grp', 'tok')), may hold values from -6 to 6
- image_positions: int32 [2, 512], P('grp', 'tok'), may hold values from 0 to 1023, as said below
- prompt_lengths: int32 [2, 2], P('grp'), may hold values from 1 to 896, 1024 in all within a row
- decoder_inproj: bfloat16 [1408, 2, 3, 704], P(('grp', 'tok'), 'sub'), may hold values from -0.15625 to 0.15625
- decoder_outproj: bfloat16 [1408, 1408], P('sub', ('grp', 'tok')), may hold values from -0.625 to 0.625
Outputs:
- text_update: bfloat16 [2048, 1408], P(('grp', 'tok', 'sub'))
Inputs may be any that keep to these rules, and one draw needn't show every extreme that they name: `image_positions`: within each half the positions are distinct. Of the 64 merged tokens of one piece, at most 16 go to positions of any one block of 128 positions, and some reach that number. `image_sizes`: each row sums to 64. `prompt_lengths`: each row sums to 1024.
All inputs are finite; a program needn't handle non-finite values.
Results may differ from a plain program's by a relative error of at most 0.03.
Values may be sent and summed in bfloat16 or wider, within the bound.
A program may use at most 128 MiB of HBM per device.

v0:
```python
import math

import jax
import jax.numpy as jnp
from jax import lax
from jax.sharding import PartitionSpec as P

HD = 88
REACH = 3


norm_eps = 1e-06


def passed_along(block, axis, distance):
    devices = range(lax.axis_size(axis))
    route = [(i - distance, i) for i in devices if i - distance in devices]
    return lax.ppermute(block, axis, route)


def layer_norm(values):
    center = values - jnp.mean(values, axis=-1, keepdims=True)
    spread = jnp.mean(center * center, axis=-1, keepdims=True)
    return center * lax.rsqrt(spread + norm_eps)


def softmax_heads(queries, keys_all, values_all, allowed):
    scores = jnp.einsum("qhe,khe->hqk", queries, keys_all, preferred_element_type=jnp.float32) * (
        1.0 / math.sqrt(HD)
    )
    weights_raw = jnp.exp(scores) * allowed[None]
    weights = (weights_raw / jnp.sum(weights_raw, axis=-1, keepdims=True)).astype(jnp.bfloat16)
    mixture = jnp.einsum("hqk,khe->qhe", weights, values_all, preferred_element_type=jnp.float32)
    return mixture.astype(jnp.bfloat16)


def attend_blocks(queries, keys_all, values_all, allowed):
    row_total, head_count, head_size = queries.shape
    block_rows = min(row_total, 512)
    block_count = row_total // block_rows
    query_blocks = queries.reshape(block_count, block_rows, head_count, head_size)
    allow_blocks = allowed.reshape(block_count, block_rows, allowed.shape[1])
    outputs = lax.map(
        lambda block_pair: softmax_heads(block_pair[0], keys_all, values_all, block_pair[1]),
        (query_blocks, allow_blocks),
    )
    return outputs.reshape(row_total, head_count * head_size)


def shards(
    patches,
    image_sizes,
    vision_inproj,
    vision_outproj,
    merger_weight,
    text_embed,
    image_positions,
    prompt_lengths,
    decoder_inproj,
    decoder_outproj,
):
    inproj_full, outproj_full, merger_full = (
        lax.all_gather(vision_inproj, "tok", axis=0, tiled=True),
        lax.all_gather(vision_outproj, "tok", axis=1, tiled=True),
        lax.all_gather(merger_weight, "tok", axis=0, tiled=True),
    )
    patch_count, width = patches.shape
    half_width = inproj_full.shape[3]
    head_local = half_width // HD
    patch_rows = patches.astype(jnp.float32)
    normed = layer_norm(patch_rows).astype(jnp.bfloat16)
    projected = jnp.dot(
        normed, inproj_full.reshape(width, 3 * half_width), preferred_element_type=jnp.float32
    )
    triple = projected.astype(jnp.bfloat16).reshape(patch_count, 3, head_local, HD)
    image_ends = jnp.cumsum(image_sizes[0])
    group_ids = jnp.arange(patch_count, dtype=jnp.int32) // 4
    image_ids = jnp.sum((group_ids[:, None] >= image_ends[None, :]).astype(jnp.int32), axis=1)
    same_image = (image_ids[:, None] == image_ids[None, :]).astype(jnp.float32)
    heads_out = attend_blocks(triple[:, 0], triple[:, 1], triple[:, 2], same_image)
    partial_value = jnp.dot(heads_out, outproj_full, preferred_element_type=jnp.float32)
    hidden = patch_rows + lax.psum(partial_value.astype(jnp.bfloat16), "sub").astype(jnp.float32)
    merged = layer_norm(hidden).astype(jnp.bfloat16).reshape(patch_count // 4, 4 * width)
    piece_count = lax.axis_size("tok")
    capacity = patch_count // (2 * piece_count)
    piece_rows = text_embed.shape[0]
    targets = image_positions[0]
    target_chip = targets // piece_rows
    target_row = targets % piece_rows
    chip_hits = (target_chip[:, None] == jnp.arange(piece_count, dtype=jnp.int32)[None, :]).astype(
        jnp.int32
    )
    slot_index = jnp.sum((jnp.cumsum(chip_hits, axis=0) - chip_hits) * chip_hits, axis=1)
    row_buffer = (
        jnp.full((piece_count, capacity), piece_rows, jnp.int32)
        .at[target_chip, slot_index]
        .set(target_row)
    )
    embedded = jnp.dot(merged, merger_full, preferred_element_type=jnp.float32).astype(jnp.bfloat16)
    narrow_rows = lax.all_to_all(
        jnp.zeros((piece_count, capacity, embedded.shape[1]), embedded.dtype)
        .at[target_chip, slot_index]
        .set(embedded),
        "tok",
        split_axis=0,
        concat_axis=0,
        tiled=True,
    )
    arrived_rows = lax.all_to_all(row_buffer, "tok", split_axis=0, concat_axis=0, tiled=True)
    image_half = narrow_rows.reshape(piece_count * capacity, half_width)
    image_full = lax.all_gather(image_half, "sub", axis=1, tiled=True)
    decoder_input = text_embed.at[arrived_rows.reshape(-1)].set(image_full, mode="drop")
    text_inproj, text_outproj = (
        lax.all_gather(decoder_inproj, ("grp", "tok"), axis=0, tiled=True),
        lax.all_gather(decoder_outproj, ("grp", "tok"), axis=1, tiled=True),
    )
    normed_text = layer_norm(decoder_input.astype(jnp.float32)).astype(jnp.bfloat16)
    text_proj = jnp.dot(
        normed_text, text_inproj.reshape(width, 3 * half_width), preferred_element_type=jnp.float32
    )
    text_triple = text_proj.astype(jnp.bfloat16).reshape(piece_rows, 3, head_local, HD)
    own_pair = text_triple[:, 1:].reshape(piece_rows, 2 * half_width)
    earlier = [own_pair]
    carried = own_pair
    for step_back in range(REACH):
        carried = passed_along(carried, "tok", 1)
        earlier.append(carried)
    window = jnp.concatenate(earlier[::-1], axis=0).reshape(
        (REACH + 1) * piece_rows, 2, head_local, HD
    )
    piece_id = lax.axis_index("tok")
    query_pos = piece_id * piece_rows + jnp.arange(piece_rows, dtype=jnp.int32)
    key_pos = (piece_id - REACH) * piece_rows + jnp.arange(
        (REACH + 1) * piece_rows, dtype=jnp.int32
    )
    lengths = prompt_lengths[0]
    starts = jnp.cumsum(lengths) - lengths
    query_start = jnp.max(
        jnp.where(starts[None, :] <= query_pos[:, None], starts[None, :], 0), axis=1
    )
    allowed = (
        (key_pos[None, :] <= query_pos[:, None]) & (key_pos[None, :] >= query_start[:, None])
    ).astype(jnp.float32)
    text_heads = attend_blocks(text_triple[:, 0], window[:, 0], window[:, 1], allowed)
    text_partial = jnp.dot(text_heads, text_outproj, preferred_element_type=jnp.float32)
    return lax.psum_scatter(
        text_partial.astype(jnp.bfloat16), "sub", scatter_dimension=0, tiled=True
    )


def solution(mesh):
    placed = (
        P(("grp", "tok"), None),
        P(("grp", "tok"), None),
        P("tok", "sub", None, None),
        P("sub", "tok"),
        P("tok", "sub"),
        P(("grp", "tok"), None),
        P("grp", "tok"),
        P("grp", None),
        P(("grp", "tok"), "sub", None, None),
        P("sub", ("grp", "tok")),
    )
    return jax.shard_map(
        shards,
        mesh=mesh,
        in_specs=placed,
        out_specs=P(("grp", "tok", "sub"), None),
        check_vma=False,
    )
```

profile of v0, /device:TPU:0, one launch (start us, length us, event | category | flops | bytes accessed | tf_op | source)
XLA Modules:
  0.0 502.8 jit_solution(17244405556347411294)
XLA Ops:
  9.6 104.1 %all-gather.6.cloned.1.call-done = bf16[1408,1,3,704]{3,0,2,1:T(8,128)(2,1)} async-done(((bf16[176,1,3,704]{3,0,2,1:T(8,128)(2,1)}), bf16[1408,1,3,704]{3,0,2,1:T(8,128)(2,1)}) %all-gather.6.cloned.1.call-update) | async-done | bytes 5947408 | tf_op jit(solution)/shard_map/all_gather | solution.py:63
  113.7 9.2 %copy.27 = bf16[1408,1,3,704]{0,3,2,1:T(8,128)(2,1)} copy(bf16[1408,1,3,704]{3,0,2,1:T(8,128)(2,1)} %all-gather.6.cloned.1.call-done) | data formatting | bytes 11894784 | tf_op jit(solution)/shard_map/all_gather | solution.py:63
  122.9 4.7 convolution_convert_fusion
  128.8 35.3 %all-gather.8.cloned.1.call-done = bf16[704,1408]{0,1:T(8,128)(2,1)} async-done(((bf16[704,176]{0,1:T(8,128)(2,1)}), bf16[704,1408]{0,1:T(8,128)(2,1)}) %all-gather.8.cloned.1.call-update) | async-done | bytes 1982480 | tf_op jit(solution)/shard_map/all_gather | solution.py:64
  164.1 3.3 convolution_convert_fusion.2
  169.6 10.2 %scatter_fusion = s32[8,16]{1,0:T(8,128)} fusion(s32[8,16]{1,0:T(8,128)} %broadcast_in_dim.19, s32[64]{0:T(128)S(1)} %fusion.24, s32[64]{0:T(128)S(1)} %get-tuple-element.27), kind=kCustom, calls=%fused_computation | custom fusion | bytes 1280 | tf_op jit(solution)/shard_map/scatter | solution.py:97
  179.8 3.3 all-to-all-start
  188.9 128.1 %all-gather.10.cloned.1.call-done = bf16[5632,704]{1,0:T(8,128)(2,1)} async-done(((bf16[704,704]{1,0:T(8,128)(2,1)}), bf16[5632,704]{1,0:T(8,128)(2,1)}) %all-gather.10.cloned.1.call-update) | async-done | bytes 7929872 | tf_op jit(solution)/shard_map/all_gather | solution.py:65
  317.0 5.1 %convolution_convert_fusion.6 = bf16[64,704]{1,0:T(8,128)(2,1)S(1)} fusion(bf16[64,5632]{1,0:T(8,128)(2,1)S(1)} %reshape.276, bf16[5632,704]{1,0:T(8,128)(2,1)} %all-gather.10.cloned.1.call-done), kind=kOutput, calls=%fused_computation.27 | convolution fusion | flops 507555840 | bytes 8740864 | tf_op jit(solution)/shard_map/dot_general | solution.py:99
  322.8 10.4 %scatter_fusion.1 = bf16[8,16,704]{2,1,0:T(8,128)(2,1)} fusion(bf16[8,16,704]{2,1,0:T(8,128)(2,1)} %broadcast_in_dim.20, s32[64]{0:T(128)S(1)} %fusion.24, bf16[64,704]{1,0:T(8,128)(2,1)S(1)} %convolution_convert_fusion.6), kind=kCustom, calls=%fused_computation.1 | custom fusion | bytes 270848 | tf_op jit(solution)/shard_map/scatter | solution.py:103
  333.2 3.4 all-to-all-start.1
  337.9 78.7 %all-gather.12.cloned.1.call-done = bf16[1408,1,3,704]{3,0,2,1:T(8,128)(2,1)} async-done(((bf16[88,1,3,704]{3,0,2,1:T(8,128)(2,1)}), bf16[1408,1,3,704]{3,0,2,1:T(8,128)(2,1)}) %all-gather.12.cloned.1.call-update) | async-done | bytes 5947408 | tf_op jit(solution)/shard_map/all_gather | solution.py:114
  416.6 9.3 %copy.31 = bf16[1408,1,3,704]{0,3,2,1:T(8,128)(2,1)} copy(bf16[1408,1,3,704]{3,0,2,1:T(8,128)(2,1)} %all-gather.12.cloned.1.call-done) | data formatting | bytes 11894784 | tf_op jit(solution)/shard_map/all_gather | solution.py:114
  426.0 2.1 all_gather.21
  430.3 4.5 convolution_convert_fusion.1
  434.8 3.4 collective-permute-start
  438.2 9.9 %collective-permute-done = bf16[128,1408]{0,1:T(8,128)(2,1)S(1)} collective-permute-done((bf16[128,1408]{0,1:T(8,128)(2,1)S(1)}, bf16[128,1408]{0,1:T(8,128)(2,1)S(1)}, u32[]{:S(2)}, u32[]{:S(2)}) %collective-permute-start) | collective-permute-done | bytes 360480 | tf_op jit(solution)/shard_map/ppermute | solution.py:18
  448.1 4.4 collective-permute-start.1
  452.7 7.0 %collective-permute-done.1 = bf16[128,1408]{0,1:T(8,128)(2,1)S(1)} collective-permute-done((bf16[128,1408]{0,1:T(8,128)(2,1)S(1)}, bf16[128,1408]{0,1:T(8,128)(2,1)S(1)}, u32[]{:S(2)}, u32[]{:S(2)}) %collective-permute-start.1) | collective-permute-done | bytes 360480 | tf_op jit(solution)/shard_map/ppermute | solution.py:18
  459.7 4.4 collective-permute-start.2
  464.3 12.8 %collective-permute-done.2 = bf16[128,1408]{0,1:T(8,128)(2,1)S(1)} collective-permute-done((bf16[128,1408]{0,1:T(8,128)(2,1)S(1)}, bf16[128,1408]{0,1:T(8,128)(2,1)S(1)}, u32[]{:S(2)}, u32[]{:S(2)}) %collective-permute-start.2) | collective-permute-done | bytes 360480 | tf_op jit(solution)/shard_map/ppermute | solution.py:18
  478.6 6.6 %all-gather.14.cloned.1.call-done = bf16[704,1408]{0,1:T(8,128)(2,1)} async-done(((bf16[704,88]{0,1:T(8,128)(2,1)}), bf16[704,1408]{0,1:T(8,128)(2,1)}) %all-gather.14.cloned.1.call-update) | async-done | bytes 1982480 | tf_op jit(solution)/shard_map/all_gather | solution.py:115
  485.2 3.2 convolution_convert_fusion.3
  488.4 7.5 %reduce-scatter.2.cloned.1.call-done = bf16[64,1408]{1,0:T(8,128)(2,1)} async-done(((bf16[128,1408]{1,0:T(8,128)(2,1)}), bf16[64,1408]{1,0:T(8,128)(2,1)}) %reduce-scatter.2.cloned.1.call-update) | async-done | bytes 180240 | tf_op jit(solution)/shard_map/reduce_scatter | solution.py:146
  (71 shorter events, 18.5 us)
Async XLA Ops:
  6.5 2.4 copy-start.1
  6.5 107.2 %all-gather.6.cloned.1.call-start = ((), (), s32[]{:S(2)}) async-start(), calls=%async_computation.3 | async-start | bytes 7299072 | tf_op jit(solution)/shard_map/all_gather | solution.py:63
  7.3 156.8 %all-gather.8.cloned.1.call-start = ((), (), s32[]{:S(2)}) async-start(), calls=%async_computation.4 | async-start | bytes 2433024 | tf_op jit(solution)/shard_map/all_gather | solution.py:64
  8.0 177.2 %all-reduce.2.cloned.1.call-start = ((), (), s32[]{:S(2)}) async-start(), calls=%async_computation.5 | async-start | bytes 1441792 | tf_op jit(solution)/shard_map/psum | solution.py:82
  164.1 4.5 copy-start.3
  167.4 149.6 %all-gather.10.cloned.1.call-start = ((), (), s32[]{:S(2)}) async-start(), calls=%async_computation.6 | async-start | bytes 9732096 | tf_op jit(solution)/shard_map/all_gather | solution.py:65
  168.0 248.6 %all-gather.12.cloned.1.call-start = ((), (), s32[]{:S(2)}) async-start(), calls=%async_computation.7 | async-start | bytes 6893568 | tf_op jit(solution)/shard_map/all_gather | solution.py:114
  179.8 153.4 %all-to-all-start = ((s32[8,1,16]{2,1,0:T(1,128)}), s32[8,1,16]{2,1,0:T(1,128)S(1)}, u32[]{:S(2)}, u32[]{:S(2)}) async-start(s32[8,1,16]{2,1,0:T(1,128)} %bitcast.5), calls=%async_computation | async-start | bytes 8192 | tf_op jit(solution)/shard_map/all_to_all | solution.py:109
  183.1 302.1 %all-gather.14.cloned.1.call-start = ((), (), s32[]{:S(2)}) async-start(), calls=%async_computation.8 | async-start | bytes 2297856 | tf_op jit(solution)/shard_map/all_gather | solution.py:115
  185.2 3.0 copy-start.2
  333.2 92.7 %all-to-all-start.1 = ((bf16[8,16,704]{2,1,0:T(8,128)(2,1)}), bf16[8,16,704]{2,1,0:T(8,128)(2,1)S(1)}, u32[]{:S(2)}, u32[]{:S(2)}) async-start(bf16[8,16,704]{2,1,0:T(8,128)(2,1)} %scatter_fusion.1), calls=%async_computation.1 | async-start | bytes 393216 | tf_op jit(solution)/shard_map/all_to_all | solution.py:100
  336.6 159.3 %reduce-scatter.2.cloned.1.call-start = ((), (), s32[]{:S(2)}) async-start(), calls=%async_computation.9 | async-start | bytes 540672 | tf_op jit(solution)/shard_map/reduce_scatter | solution.py:146
  425.9 2.4 copy-start
  430.2 22.2 %copy-start.4 = (s32[1,2]{1,0:T(1,128)S(1)}, s32[1,2]{1,0:T(1,128)}, u32[]{:S(2)}) copy-start(s32[1,2]{1,0:T(1,128)} %param.17) | copy-start | bytes 28
  434.8 13.3 %collective-permute-start = (bf16[128,1408]{0,1:T(8,128)(2,1)S(1)}, bf16[128,1408]{0,1:T(8,128)(2,1)S(1)}, u32[]{:S(2)}, u32[]{:S(2)}) collective-permute-start(bf16[128,1408]{0,1:T(8,128)(2,1)S(1)} %bitcast.95), channel_id=1, source_target_pairs={{0,2},{2,4},{4,6},{6,8},{8,10},{10,12},{12,14},{1,3},{3,5},{5,7},{... | collective-permute-start | bytes 1081352 | tf_op jit(solution)/shard_map/ppermute | solution.py:18
  448.1 11.6 %collective-permute-start.1 = (bf16[128,1408]{0,1:T(8,128)(2,1)S(1)}, bf16[128,1408]{0,1:T(8,128)(2,1)S(1)}, u32[]{:S(2)}, u32[]{:S(2)}) collective-permute-start(bf16[128,1408]{0,1:T(8,128)(2,1)S(1)} %collective-permute-done), channel_id=1, source_target_pairs={{0,2},{2,4},{4,6},{6,8},{8,10},{10,12},{12,14},{1,3},{3,5},{5,7},{... | collective-permute-start | bytes 1081352 | tf_op jit(solution)/shard_map/ppermute | solution.py:18
  459.7 17.4 %collective-permute-start.2 = (bf16[128,1408]{0,1:T(8,128)(2,1)S(1)}, bf16[128,1408]{0,1:T(8,128)(2,1)S(1)}, u32[]{:S(2)}, u32[]{:S(2)}) collective-permute-start(bf16[128,1408]{0,1:T(8,128)(2,1)S(1)} %collective-permute-done.1), channel_id=1, source_target_pairs={{0,2},{2,4},{4,6},{6,8},{8,10},{10,12},{12,14},{1,3},{3,5},{5,7},{... | collective-permute-start | bytes 1081352 | tf_op jit(solution)/shard_map/ppermute | solution.py:18
Sparse Core Ops, SparseCore 0:
  9.5 104.1 all-gather.5
  115.9 48.1 all-gather.7
  167.5 17.6 all-reduce.1
  187.5 129.5 all-gather.9
  320.1 96.4 all-gather.11
  419.5 65.6 all-gather.13
  488.5 7.3 reduce-scatter.1
where the time goes:
time: 504 us; the launch traced here: 503 us
  waiting for transfers between devices  394 us (78%)
  local copies, waits for them, and re-layouts  43.3 us (9%)
  matrix products  23.3 us (5%)
  starting transfers between devices  19.1 us (4%)
  between operations  13.7 us (3%)
  other arithmetic  6.76 us (1%)
    all_gather x1, waiting for transfers between devices, shards(): lax.all_gather(merger_weight, 'tok', axis=0, tiled=True)  128 us
    all_gather x1, waiting for transfers between devices, shards(): lax.all_gather(vision_inproj, 'tok', axis=0, tiled=True)  104 us
    all_gather x1, waiting for transfers between devices, shards(): lax.all_gather(decoder_inproj, ('grp', 'tok'), axis=0, tiled=True)  78.7 us
    all_gather x1, waiting for transfers between devices, shards(): lax.all_gather(vision_outproj, 'tok', axis=1, tiled=True)  35.3 us
    ppermute x3, waiting for transfers between devices, passed_along(): return lax.ppermute(block, axis, route)  29.6 us
    ppermute x3, starting transfers between devices, passed_along(): return lax.ppermute(block, axis, route)  12.2 us
    scatter x1, local copies, waits for them, and re-layouts, shards(): narrow_rows = lax.all_to_all(jnp.zeros((piece_count, capacity, embedded.s...  10.4 us
    scatter x1, local copies, waits for them, and re-layouts, shards(): row_buffer = jnp.full((piece_count, capacity), piece_rows, jnp.int32).at[...  10.2 us
  transfers between devices with their start and end apart: 12, of which 10 were waited for; matrix products, arithmetic and copies ran while one was open for 13% of the time, Pallas kernels for 0%

commit v1 on v0

--- a/solution.py
+++ b/solution.py
@@ -1,8 +1,11 @@
+import functools
 import math
 
 import jax
 import jax.numpy as jnp
 from jax import lax
+from jax.experimental import pallas as pl
+from jax.experimental.pallas import tpu as pltpu
 from jax.sharding import PartitionSpec as P
 
 HD = 88
@@ -47,7 +50,7 @@
     return outputs.reshape(row_total, head_count * head_size)
 
 
-def shards(
+def shards_general(
     patches,
     image_sizes,
     vision_inproj,
@@ -148,6 +151,328 @@
     )
 
 
+LANES = 128
+MESH = pl.DeviceIdType.MESH
+
+
+def head_kernel(
+    kind, n_tok, x_ref, w_ref, info_ref, out_ref, buf, staged, kv, send_sem, recv_sem, back_send, back_recv
+):
+    me, core = lax.axis_index("tok"), lax.axis_index("sub")
+    rows = 2 * x_ref.shape[0]
+    z, y = lax.div(me, 2), lax.rem(me, 2)
+    n_z = n_tok // 2
+    side = me + 1 - 2 * y
+
+    barrier = pltpu.get_barrier_semaphore()
+    for d in range(1, n_tok):
+        pl.semaphore_signal(
+            barrier, inc=1, device_id={"tok": lax.rem(me + d, n_tok)}, device_id_type=MESH
+        )
+    pl.semaphore_signal(barrier, inc=1, device_id={"sub": 1 - core}, device_id_type=MESH)
+
+    own = x_ref[...].astype(jnp.float32)
+    buf[me, core] = layer_norm(own).astype(jnp.bfloat16)
+    pl.semaphore_wait(barrier, n_tok)
+
+    def push(t, way):
+        target = [{"tok": me + 2}, {"tok": me - 2}, {"tok": side}, {"sub": 1 - core}][way]
+        return pltpu.make_async_remote_copy(
+            src_ref=buf.at[t, core],
+            dst_ref=buf.at[t, core],
+            send_sem=send_sem.at[way, t],
+            recv_sem=recv_sem.at[t, core],
+            device_id=target,
+            device_id_type=MESH,
+        )
+
+    def arrived(t, c):
+        pltpu.make_async_remote_copy(
+            src_ref=buf.at[t, c],
+            dst_ref=buf.at[t, c],
+            send_sem=send_sem.at[3, t],
+            recv_sem=recv_sem.at[t, c],
+            device_id={"sub": 1 - core},
+            device_id_type=MESH,
+        ).wait_recv()
+
+    def run(act, wait):
+        @pl.when(z < n_z - 1)
+        def _():
+            act(me, 0)
+
+        @pl.when(z > 0)
+        def _():
+            act(me, 1)
+
+        act(me, 2)
+        act(me, 3)
+        for k in range(1, n_z + 1):
+            if k < n_z:
+                @pl.when(z - k >= 0)
+                def _():
+                    wait(me - 2 * k)
+
+                    @pl.when(z < n_z - 1)
+                    def _():
+                        act(me - 2 * k, 0)
+
+                    act(me - 2 * k, 2)
+                    act(me - 2 * k, 3)
+
+                @pl.when(z + k < n_z)
+                def _():
+                    wait(me + 2 * k)
+
+                    @pl.when(z > 0)
+                    def _():
+                        act(me + 2 * k, 1)
+
+                    act(me + 2 * k, 2)
+                    act(me + 2 * k, 3)
+            if k == 1:
+                wait(side)
+                act(side, 3)
+            else:
+                @pl.when(z - k + 1 >= 0)
+                def _():
+                    wait(side - 2 * k + 2)
+                    act(side - 2 * k + 2, 3)
+
+                @pl.when(z + k - 1 < n_z)
+                def _():
+                    wait(side + 2 * k - 2)
+                    act(side + 2 * k - 2, 3)
+
+    run(lambda t, way: push(t, way).start(), lambda t: arrived(t, core))
+    for t in range(n_tok):
+        arrived(t, 1 - core)
+
+    def project(j):
+        block = buf[j].reshape(rows, buf.shape[3])
+        return jnp.dot(block, w_ref[...], preferred_element_type=jnp.float32).astype(jnp.bfloat16)
+
+    def mix(query, key, value, allowed):
+        scores = lax.dot_general(
+            query, key, (((1,), (1,)), ((), ())), preferred_element_type=jnp.float32
+        ) * (1.0 / math.sqrt(HD))
+        raw = jnp.where(allowed, jnp.exp(scores), 0.0)
+        weights = (raw / jnp.sum(raw, axis=-1, keepdims=True)).astype(jnp.bfloat16)
+        return jnp.dot(weights, value, preferred_element_type=jnp.float32).astype(jnp.bfloat16)
+
+    def back(j):
+        return pltpu.make_async_remote_copy(
+            src_ref=staged.at[j],
+            dst_ref=out_ref.at[me],
+            send_sem=back_send.at[j],
+            recv_sem=back_recv.at[me],
+            device_id={"tok": j},
+            device_id_type=MESH,
+        )
+
+    if kind == "text":
+        kv[pl.ds(0, REACH)] = jnp.zeros((REACH, rows, 3 * LANES), jnp.bfloat16)
+
+        def fill(j, carry):
+            kv[j + REACH] = project(j)
+            return carry
+
+        lax.fori_loop(0, n_tok, fill, 0)
+
+    def piece(d, carry):
+        j = lax.rem(me + d, n_tok)
+        if kind == "image":
+            proj = project(j)
+            query, key, value = (proj[:, i * LANES : (i + 1) * LANES] for i in range(3))
+            left = lax.div(lax.broadcasted_iota(jnp.int32, (rows, 1), 0), 4)
+            right = lax.div(lax.broadcasted_iota(jnp.int32, (1, rows), 1), 4)
+            left_id, right_id = jnp.zeros_like(left), jnp.zeros_like(right)
+            for i in range(info_ref.shape[1]):
+                end = info_ref[j, i]
+                left_id = left_id + jnp.where(left >= end, 1, 0)
+                right_id = right_id + jnp.where(right >= end, 1, 0)
+            allowed = left_id == right_id
+        else:
+            span = (REACH + 1) * rows
+            query = kv[j + REACH, :, 0:LANES]
+            key = kv[pl.ds(j, REACH + 1), :, LANES : 2 * LANES].reshape(span, LANES)
+            value = kv[pl.ds(j, REACH + 1), :, 2 * LANES : 3 * LANES].reshape(span, LANES)
+            query_pos = j * rows + lax.broadcasted_iota(jnp.int32, (rows, 1), 0)
+            key_pos = (j - REACH) * rows + lax.broadcasted_iota(jnp.int32, (1, span), 1)
+            begin = jnp.zeros_like(query_pos)
+            for i in range(info_ref.shape[1]):
+                first = info_ref[0, i]
+                begin = jnp.maximum(begin, jnp.where(query_pos >= first, first, 0))
+            allowed = (key_pos <= query_pos) & (key_pos >= begin)
+        mixture = mix(query, key, value, allowed)
+
+        @pl.when(d < n_tok)
+        def _():
+            staged[j] = mixture
+            back(j).start()
+
+        @pl.when(d == n_tok)
+        def _():
+            out_ref[me] = mixture
+
+        return carry
+
+    lax.fori_loop(1, n_tok + 1, piece, 0)
+
+    run(lambda t, way: push(t, way).wait_send(), lambda t: None)
+    for d in range(1, n_tok):
+        j = lax.rem(me + d, n_tok)
+        back(j).wait_send()
+        pltpu.make_async_remote_copy(
+            src_ref=staged.at[j],
+            dst_ref=out_ref.at[j],
+            send_sem=back_send.at[j],
+            recv_sem=back_recv.at[j],
+            device_id={"tok": j},
+            device_id_type=MESH,
+        ).wait_recv()
+
+
+def heads_of(kind, half_rows, weight, info, n_tok):
+    half, width = half_rows.shape
+    rows = 2 * half
+    kv_shape = (n_tok + REACH, rows, 3 * LANES) if kind == "text" else (1, 16, LANES)
+    vmem = pl.BlockSpec(memory_space=pltpu.VMEM)
+    total = n_tok * rows
+    return pl.pallas_call(
+        functools.partial(head_kernel, kind, n_tok),
+        out_shape=jax.ShapeDtypeStruct((n_tok, rows, LANES), jnp.bfloat16),
+        in_specs=[vmem, vmem, pl.BlockSpec(memory_space=pltpu.SMEM)],
+        out_specs=vmem,
+        scratch_shapes=[
+            pltpu.VMEM((n_tok, 2, half, width), jnp.bfloat16),
+            pltpu.VMEM((n_tok, rows, LANES), jnp.bfloat16),
+            pltpu.VMEM(kv_shape, jnp.bfloat16),
+            pltpu.SemaphoreType.DMA((4, n_tok)),
+            pltpu.SemaphoreType.DMA((n_tok, 2)),
+            pltpu.SemaphoreType.DMA((n_tok,)),
+            pltpu.SemaphoreType.DMA((n_tok,)),
+        ],
+        compiler_params=pltpu.CompilerParams(
+            collective_id=0 if kind == "image" else 1,
+            has_side_effects=True,
+            vmem_limit_bytes=40 * 1024 * 1024,
+        ),
+        cost_estimate=pl.CostEstimate(
+            flops=2 * total * width * 3 * LANES, bytes_accessed=2 * total * width, transcendentals=0
+        ),
+    )(half_rows, weight, info)
+
+
+def head_columns(weight, head_local):
+    rows = weight.shape[0]
+    split = weight.reshape(rows, 3, head_local, HD).transpose(2, 0, 1, 3)
+    split = jnp.pad(split, ((0, 0), (0, 0), (0, 0), (0, LANES - HD)))
+    return split.reshape(head_local, rows, 3 * LANES)
+
+
+def head_rows(weight, head_local):
+    split = weight.reshape(head_local, HD, weight.shape[1])
+    return jnp.pad(split, ((0, 0), (0, LANES - HD), (0, 0)))
+
+
+def across(block, axis):
+    return lax.all_to_all(block, axis, split_axis=0, concat_axis=0, tiled=True)
+
+
+def shards(
+    patches,
+    image_sizes,
+    vision_inproj,
+    vision_outproj,
+    merger_weight,
+    text_embed,
+    image_positions,
+    prompt_lengths,
+    decoder_inproj,
+    decoder_outproj,
+):
+    n_tok = lax.axis_size("tok")
+    half_width = vision_inproj.shape[3]
+    head_local = half_width // HD
+    if n_tok != head_local or lax.axis_size("sub") != 2:
+        return shards_general(
+            patches,
+            image_sizes,
+            vision_inproj,
+            vision_outproj,
+            merger_weight,
+            text_embed,
+            image_positions,
+            prompt_lengths,
+            decoder_inproj,
+            decoder_outproj,
+        )
+    core = lax.axis_index("sub")
+    patch_count, width = patches.shape
+    piece_rows = text_embed.shape[0]
+    bf16, f32 = jnp.bfloat16, jnp.float32
+
+    vision_weight = across(head_columns(vision_inproj, head_local), "tok").reshape(width, 3 * LANES)
+    text_part = across(head_columns(decoder_inproj, head_local), "tok").reshape(-1, 3 * LANES)
+    text_weight = lax.all_gather(text_part, "grp", axis=0, tiled=True)
+    vision_out = head_rows(lax.all_gather(vision_outproj, "tok", axis=1, tiled=True), head_local)
+    text_out = head_rows(
+        lax.all_gather(decoder_outproj, ("grp", "tok"), axis=1, tiled=True), head_local
+    )
+
+    image_ends = lax.all_gather(jnp.cumsum(image_sizes, axis=1), "tok", axis=0, tiled=True)
+    half_patches = lax.dynamic_slice_in_dim(patches, core * (patch_count // 2), patch_count // 2, 0)
+    heads = heads_of("image", half_patches, vision_weight, image_ends, n_tok)
+    partial_value = jnp.einsum("hrc,hcn->rn", heads, vision_out, preferred_element_type=f32).astype(
+        bf16
+    )
+    other = lax.ppermute(partial_value, "sub", [(0, 1), (1, 0)])
+    hidden = patches.astype(f32) + (partial_value.astype(f32) + other.astype(f32))
+    merged = layer_norm(hidden).astype(bf16)
+
+    group_count = patch_count // 4
+    shard_depth = merger_weight.shape[0]
+    parts = 4 * width // shard_depth
+    cut = merged.reshape(group_count, 4, parts // 4, shard_depth).transpose(1, 2, 0, 3)
+    gathered = across(cut.reshape(parts, group_count, shard_depth), "tok")
+    partial_embed = jnp.dot(
+        gathered.reshape(n_tok * group_count, shard_depth), merger_weight, preferred_element_type=f32
+    ).astype(bf16)
+    embedded = jnp.sum(
+        across(partial_embed.reshape(n_tok, group_count, half_width), "tok").astype(f32), axis=0
+    ).astype(bf16)
+
+    capacity = patch_count // (2 * n_tok)
+    targets = image_positions[0]
+    target_chip = targets // piece_rows
+    target_row = targets % piece_rows
+    chip_hits = (target_chip[:, None] == jnp.arange(n_tok, dtype=jnp.int32)[None, :]).astype(jnp.int32)
+    slot_index = jnp.sum((jnp.cumsum(chip_hits, axis=0) - chip_hits) * chip_hits, axis=1)
+    slot = target_chip * capacity + slot_index
+    slot_hit = jnp.arange(n_tok * capacity, dtype=jnp.int32)[:, None] == slot[None, :]
+    row_buffer = jnp.sum(jnp.where(slot_hit, target_row[None, :] + 1, 0), axis=1) - 1
+    arrived_rows = across(row_buffer.reshape(n_tok, capacity), "tok").reshape(-1)
+    packed = jnp.dot(slot_hit.astype(bf16), embedded, preferred_element_type=f32).astype(bf16)
+    narrow_rows = across(packed.reshape(n_tok, capacity, half_width), "tok").reshape(-1, half_width)
+    row_hit = jnp.arange(piece_rows, dtype=jnp.int32)[:, None] == arrived_rows[None, :]
+    placed = jnp.dot(row_hit.astype(bf16), narrow_rows, preferred_element_type=f32).astype(bf16)
+    half_piece = piece_rows // 2
+    swapped = across(placed.reshape(2, half_piece, half_width), "sub")
+    image_rows = swapped.transpose(1, 0, 2).reshape(half_piece, width)
+    filled = lax.dynamic_slice_in_dim(
+        jnp.any(row_hit, axis=1).astype(jnp.int32), core * half_piece, half_piece, 0
+    )
+    text_half = lax.dynamic_slice_in_dim(text_embed, core * half_piece, half_piece, 0)
+    decoder_input = jnp.where(filled[:, None] > 0, image_rows, text_half)
+
+    starts = jnp.cumsum(prompt_lengths, axis=1) - prompt_lengths
+    text_heads = heads_of("text", decoder_input, text_weight, starts, n_tok)
+    text_partial = jnp.einsum("hrc,hcn->rn", text_heads, text_out, preferred_element_type=f32)
+    pair = across(text_partial.astype(bf16).reshape(2, half_piece, width), "sub")
+    return jnp.sum(pair.astype(f32), axis=0).astype(bf16)
+
+
 def solution(mesh):
     placed = (
         P(("grp", "tok"), None),

time: 504 us -> 289 us (0.57)
  waiting for transfers between devices: 394 us -> 70.4 us
  Pallas kernels: 0 us -> 90.5 us
  blocking collectives: 2.06 us -> 49 us
  matrix products: 23.3 us -> 4.5 us
  local copies, waits for them, and re-layouts: 43.3 us -> 25.2 us
  starting transfers between devices: 19.1 us -> 27.9 us
    all_gather x3 -> x1, waiting for transfers between devices: 311 us -> 0.03 us  [shards(): text_weight = lax.all_gather(text_part, 'grp', axis=0, tiled=True)]
    pallas_call x0 -> x2, Pallas kernels: none -> 90.5 us  [heads_of(): pl.pallas_call(functools.partial(head_kernel, kind, n_tok), out_shape=jax...]
    all_to_all x2 -> x6, waiting for transfers between devices: 0.01 us -> 67.8 us  [across(): return lax.all_to_all(block, axis, split_axis=0, concat_axis=0, tiled=True)]
    all_gather x1, blocking collectives: 2.06 us -> 40.6 us  [shards(): lax.all_gather(jnp.cumsum(image_sizes, axis=1), 'tok', axis=0, tiled=True)]
    all_gather x1, waiting for transfers between devices: 35.3 us -> 0.02 us  [shards(): lax.all_gather(vision_outproj, 'tok', axis=1, tiled=True)]
    ppermute x3 -> x1, waiting for transfers between devices: 29.6 us -> 1.86 us  [shards(): other = lax.ppermute(partial_value, 'sub', [(0, 1), (1, 0)])]
    scatter x3 -> x0, local copies, waits for them, and re-layouts: 22.1 us -> none  [the longest x1 10.4 us: shards(): narrow_rows = lax.all_to_all(jnp.zeros((piece_count, capacity, embedded.s...]
    all_to_all x2 -> x6, starting transfers between devices: 6.7 us -> 27.5 us  [across(): return lax.all_to_all(block, axis, split_axis=0, concat_axis=0, tiled=True)]
  transfers between devices with their start and end apart: 12 -> 10, of which waited for: 10 -> 6; matrix products, arithmetic and copies ran while one was open for 13% -> 9% of each run, Pallas kernels for 0% -> 20%
where the time goes in v1:
time: 289 us; the launch traced here: 288 us
  Pallas kernels  90.5 us (31%)
  waiting for transfers between devices  70.4 us (24%)
  blocking collectives  49 us (17%)
  starting transfers between devices  27.9 us (10%)
  local copies, waits for them, and re-layouts  25.2 us (9%)
  between operations  15.1 us (5%)
  other arithmetic  5.8 us (2%)
  matrix products  4.5 us (2%)
    pallas_call x2, Pallas kernels, heads_of(): pl.pallas_call(functools.partial(head_kernel, kind, n_tok), out_shape=jax...  90.5 us
    all_to_all x6, waiting for transfers between devices, across(): return lax.all_to_all(block, axis, split_axis=0, concat_axis=0, tiled=True)  67.8 us
    all_gather x1, blocking collectives, shards(): lax.all_gather(jnp.cumsum(image_sizes, axis=1), 'tok', axis=0, tiled=True)  40.6 us
    all_to_all x6, starting transfers between devices, across(): return lax.all_to_all(block, axis, split_axis=0, concat_axis=0, tiled=True)  27.5 us
    all_to_all x2, blocking collectives, across(): return lax.all_to_all(block, axis, split_axis=0, concat_axis=0, tiled=True)  8.34 us
  transfers between devices with their start and end apart: 10, of which 6 were waited for; matrix products, arithmetic and copies ran while one was open for 9% of the time, Pallas kernels for 20%

profile of v1, /device:TPU:0, one launch (start us, length us, event | category | flops | bytes accessed | tf_op | source)
XLA Modules:
  0.0 288.5 jit_solution(4331424591474797381)
XLA Ops:
  8.1 2.4 reshape.113
  12.2 1.7 reshape.114
  13.9 7.4 %all-to-all-start.1 = ((bf16[8,176,384]{2,1,0:T(8,128)(2,1)}), bf16[8,176,384]{2,1,0:T(8,128)(2,1)S(1)}, u32[]{:S(2)}, u32[]{:S(2)}) async-start(bf16[8,176,384]{2,1,0:T(8,128)(2,1)} %reshape.114), calls=%async_computation.1 | async-start | bytes 2162688 | tf_op jit(solution)/shard_map/all_to_all | solution.py:380
  21.6 40.6 %all-gather = s32[8,1,4]{2,1,0:T(1,128)S(1)} all-gather(s32[1,1,4]{2,1,0:T(1,128)S(1)} %bitcast.73), channel_id=1, replica_groups=mesh['grp'=2,'tok'=8,'sub'=2] {'tok'}, dimensions={0}, use_global_device_ids=true | all-gather | bytes 144 | tf_op jit(solution)/shard_map/all_gather | solution.py:424
  62.2 58.8 %shard_map.100 = bf16[8,256,128]{2,1,0:T(8,128)(2,1)S(1)} custom-call(bf16[128,1408]{1,0:T(8,128)(2,1)S(1)} %constant_dynamic-slice_fusion.x_ref, bf16[1408,384]{1,0:T(8,128)(2,1)S(1)} %bitcast.60, s32[8,4]{1,0:T(8,128)S(1)} %bitcast.61), custom_call_target="tpu_custom_call" | custom-call | flops 2214592512 | bytes 5767168 | tf_op jit(solution)/shard_map/pallas_call | solution.py:342
  121.1 4.1 %copy.45 = bf16[704,1408]{1,0:T(8,128)(2,1)} copy(bf16[704,1408]{0,1:T(8,128)(2,1)} %all-gather.5.cloned.1.call-done) | data formatting | bytes 3964928 | tf_op jit(solution)/shard_map/all_gather | solution.py:419
  125.2 2.6 fusion.7
  128.2 1.9 collective-permute-done
  130.9 1.3 multiply_convert_fusion
  132.1 2.6 reshape.117
  135.8 6.0 %all-to-all-start.2 = ((bf16[8,64,704]{2,1,0:T(8,128)(2,1)}), bf16[8,64,704]{2,1,0:T(8,128)(2,1)S(1)}, u32[]{:S(2)}, u32[]{:S(2)}) async-start(bf16[8,64,704]{2,1,0:T(8,128)(2,1)} %bitcast.12), calls=%async_computation.2 | async-start | bytes 1572864 | tf_op jit(solution)/shard_map/all_to_all | solution.py:380
  144.6 21.1 %all-to-all-done.2 = bf16[8,64,704]{2,1,0:T(8,128)(2,1)S(1)} async-done(((bf16[8,64,704]{2,1,0:T(8,128)(2,1)}), bf16[8,64,704]{2,1,0:T(8,128)(2,1)S(1)}, u32[]{:S(2)}, u32[]{:S(2)}) %all-to-all-start.2) | async-done | bytes 720928 | tf_op jit(solution)/shard_map/all_to_all | solution.py:380
  165.7 3.7 %all-to-all-start.6 = ((bf16[8,88,384]{2,1,0:T(8,128)(2,1)}), bf16[8,88,384]{2,1,0:T(8,128)(2,1)S(1)}, u32[]{:S(2)}, u32[]{:S(2)}) async-start(bf16[8,88,384]{2,1,0:T(8,128)(2,1)} %reshape.126), calls=%async_computation.6 | async-start | bytes 1081344 | tf_op jit(solution)/shard_map/all_to_all | solution.py:380
  171.3 15.6 %all-to-all-done.6 = bf16[8,88,384]{2,1,0:T(8,128)(2,1)S(1)} async-done(((bf16[8,88,384]{2,1,0:T(8,128)(2,1)}), bf16[8,88,384]{2,1,0:T(8,128)(2,1)S(1)}, u32[]{:S(2)}, u32[]{:S(2)}) %all-to-all-start.6) | async-done | bytes 540704 | tf_op jit(solution)/shard_map/all_to_all | solution.py:380
  187.0 3.6 %all-to-all-start.3 = ((bf16[8,64,704]{2,1,0:T(8,128)(2,1)}), bf16[8,64,704]{2,1,0:T(8,128)(2,1)S(1)}, u32[]{:S(2)}, u32[]{:S(2)}) async-start(bf16[8,64,704]{2,1,0:T(8,128)(2,1)} %bitcast.14), calls=%async_computation.3 | async-start | bytes 1572864 | tf_op jit(solution)/shard_map/all_to_all | solution.py:380
  191.9 22.9 %all-to-all-done.3 = bf16[8,64,704]{2,1,0:T(8,128)(2,1)S(1)} async-done(((bf16[8,64,704]{2,1,0:T(8,128)(2,1)}), bf16[8,64,704]{2,1,0:T(8,128)(2,1)S(1)}, u32[]{:S(2)}, u32[]{:S(2)}) %all-to-all-start.3) | async-done | bytes 720928 | tf_op jit(solution)/shard_map/all_to_all | solution.py:380
  214.8 3.4 %all-to-all-start = ((s32[8,1,16]{2,1,0:T(1,128)}), s32[8,1,16]{2,1,0:T(1,128)S(1)}, u32[]{:S(2)}, u32[]{:S(2)}) async-start(s32[8,1,16]{2,1,0:T(1,128)} %bitcast.4), calls=%async_computation | async-start | bytes 8192 | tf_op jit(solution)/shard_map/all_to_all | solution.py:380
  219.4 5.2 %all-to-all-done = s32[8,1,16]{2,1,0:T(1,128)S(1)} async-done(((s32[8,1,16]{2,1,0:T(1,128)}), s32[8,1,16]{2,1,0:T(1,128)S(1)}, u32[]{:S(2)}, u32[]{:S(2)}) %all-to-all-start) | async-done | bytes 544 | tf_op jit(solution)/shard_map/all_to_all | solution.py:380
  224.6 3.4 %all-to-all-start.4 = ((bf16[8,16,704]{2,1,0:T(8,128)(2,1)}), bf16[8,16,704]{2,1,0:T(8,128)(2,1)S(1)}, u32[]{:S(2)}, u32[]{:S(2)}) async-start(bf16[8,16,704]{2,1,0:T(8,128)(2,1)} %bitcast.15), calls=%async_computation.4 | async-start | bytes 393216 | tf_op jit(solution)/shard_map/all_to_all | solution.py:380
  229.7 3.1 %copy.52 = bf16[704,1408]{1,0:T(8,128)(2,1)S(1)} copy(bf16[704,1408]{0,1:T(8,128)(2,1)} %all-gather.9.cloned.1.call-done) | data formatting | bytes 3964928 | tf_op jit(solution)/shard_map/all_gather | solution.py:421
  232.8 2.9 %all-to-all-done.4 = bf16[8,16,704]{2,1,0:T(8,128)(2,1)S(1)} async-done(((bf16[8,16,704]{2,1,0:T(8,128)(2,1)}), bf16[8,16,704]{2,1,0:T(8,128)(2,1)S(1)}, u32[]{:S(2)}, u32[]{:S(2)}) %all-to-all-start.4) | async-done | bytes 180256 | tf_op jit(solution)/shard_map/all_to_all | solution.py:380
  236.1 3.9 %all_to_all.41 = bf16[2,64,704]{2,1,0:T(8,128)(2,1)S(1)} all-to-all(bf16[2,64,704]{2,1,0:T(8,128)(2,1)S(1)} %bitcast.70), channel_id=1, replica_groups=mesh['grp'=2,'tok'=8,'sub'=2] {'sub'}, dimensions={0} | all-to-all | bytes 360448 | tf_op jit(solution)/shard_map/all_to_all | solution.py:380
  243.5 31.7 %shard_map.101 = bf16[8,128,128]{2,1,0:T(8,128)(2,1)S(1)} custom-call(bf16[64,1408]{1,0:T(8,128)(2,1)S(1)} %dynamic-slice_select_fusion.x_ref, bf16[1408,384]{1,0:T(8,128)(2,1)S(1)} %copy-done.1, s32[1,2]{1,0:T(1,128)S(1)} %sub.35.info_ref), custom_call_target="tpu_custom_call" | custom-call | flops 1107296256 | bytes 2883584 | tf_op jit(solution)/shard_map/pallas_call | solution.py:342
  275.8 4.4 %all_to_all.42 = bf16[2,64,1408]{2,1,0:T(8,128)(2,1)S(1)} all-to-all(bf16[2,64,1408]{2,1,0:T(8,128)(2,1)S(1)} %bitcast.72), channel_id=1, replica_groups=mesh['grp'=2,'tok'=8,'sub'=2] {'sub'}, dimensions={0} | all-to-all | bytes 720896 | tf_op jit(solution)/shard_map/all_to_all | solution.py:380
  (70 shorter events, 18.9 us)
Async XLA Ops:
  7.4 162.0 %copy-start = (bf16[704,704]{1,0:T(8,128)(2,1)S(1)}, bf16[704,704]{1,0:T(8,128)(2,1)}, u32[]{:S(2)}) copy-start(bf16[704,704]{1,0:T(8,128)(2,1)} %param.14) | copy-start | bytes 2973700
  7.4 113.7 %all-gather.5.cloned.1.call-start = ((), (), s32[]{:S(2)}) async-start(), calls=%async_computation.8 | async-start | bytes 2433024 | tf_op jit(solution)/shard_map/all_gather | solution.py:419
  13.9 7.5 %copy-start.7 = (s32[1,4]{1,0:T(1,128)S(1)}, s32[1,4]{1,0:T(1,128)}, u32[]{:S(2)}) copy-start(s32[1,4]{1,0:T(1,128)} %param.11) | copy-start | bytes 52
  13.9 48.3 %copy-start.2 = (bf16[256,1408]{1,0:T(8,128)(2,1)S(1)}, bf16[256,1408]{1,0:T(8,128)(2,1)}, u32[]{:S(2)}) copy-start(bf16[256,1408]{1,0:T(8,128)(2,1)} %param.10) | copy-start | bytes 2162692
  13.9 48.3 %all-to-all-start.1 = ((bf16[8,176,384]{2,1,0:T(8,128)(2,1)}), bf16[8,176,384]{2,1,0:T(8,128)(2,1)S(1)}, u32[]{:S(2)}, u32[]{:S(2)}) async-start(bf16[8,176,384]{2,1,0:T(8,128)(2,1)} %reshape.114), calls=%async_computation.1 | async-start | bytes 2162688 | tf_op jit(solution)/shard_map/all_to_all | solution.py:380
  21.3 208.3 %all-gather.9.cloned.1.call-start = ((), (), s32[]{:S(2)}) async-start(), calls=%async_computation.10 | async-start | bytes 2297856 | tf_op jit(solution)/shard_map/all_gather | solution.py:421
  125.2 4.9 %copy-start.3 = (bf16[256,1408]{1,0:T(8,128)(2,1)S(1)}, bf16[256,1408]{1,0:T(8,128)(2,1)}, u32[]{:S(2)}) copy-start(bf16[256,1408]{1,0:T(8,128)(2,1)} %param.10) | copy-start | bytes 2162692
  127.8 2.3 collective-permute-start
  134.8 7.0 %copy-start.5 = (bf16[88,1,3,704]{3,0,2,1:T(8,128)(2,1)S(1)}, bf16[88,1,3,704]{3,0,2,1:T(8,128)(2,1)}, u32[]{:S(2)}) copy-start(bf16[88,1,3,704]{3,0,2,1:T(8,128)(2,1)} %param.18) | copy-start | bytes 1115140
  135.8 29.9 %all-to-all-start.2 = ((bf16[8,64,704]{2,1,0:T(8,128)(2,1)}), bf16[8,64,704]{2,1,0:T(8,128)(2,1)S(1)}, u32[]{:S(2)}, u32[]{:S(2)}) async-start(bf16[8,64,704]{2,1,0:T(8,128)(2,1)} %bitcast.12), calls=%async_computation.2 | async-start | bytes 1572864 | tf_op jit(solution)/shard_map/all_to_all | solution.py:380
  165.7 21.3 %all-to-all-start.6 = ((bf16[8,88,384]{2,1,0:T(8,128)(2,1)}), bf16[8,88,384]{2,1,0:T(8,128)(2,1)S(1)}, u32[]{:S(2)}, u32[]{:S(2)}) async-start(bf16[8,88,384]{2,1,0:T(8,128)(2,1)} %reshape.126), calls=%async_computation.6 | async-start | bytes 1081344 | tf_op jit(solution)/shard_map/all_to_all | solution.py:380
  170.2 20.5 %copy-start.6 = (s32[1,64]{1,0:T(1,128)S(1)}, s32[1,64]{1,0:T(1,128)}, u32[]{:S(2)}) copy-start(s32[1,64]{1,0:T(1,128)} %param.16) | copy-start | bytes 772
  187.0 4.9 %copy-start.4 = (bf16[8,88,384]{2,1,0:T(8,128)(2,1)}, bf16[8,88,384]{2,1,0:T(8,128)(2,1)S(1)}, u32[]{:S(2)}) copy-start(bf16[8,88,384]{2,1,0:T(8,128)(2,1)S(1)} %all-to-all-done.6) | copy-start | bytes 1622020
  187.0 27.8 %all-to-all-start.3 = ((bf16[8,64,704]{2,1,0:T(8,128)(2,1)}), bf16[8,64,704]{2,1,0:T(8,128)(2,1)S(1)}, u32[]{:S(2)}, u32[]{:S(2)}) async-start(bf16[8,64,704]{2,1,0:T(8,128)(2,1)} %bitcast.14), calls=%async_computation.3 | async-start | bytes 1572864 | tf_op jit(solution)/shard_map/all_to_all | solution.py:380
  190.6 37.4 %copy-start.8 = (s32[1,2]{1,0:T(1,128)S(1)}, s32[1,2]{1,0:T(1,128)}, u32[]{:S(2)}) copy-start(s32[1,2]{1,0:T(1,128)} %param.17) | copy-start | bytes 28
  190.6 51.6 %all-gather.7.cloned.1.call-start = ((), (), s32[]{:S(2)}) async-start(), calls=%async_computation.9 | async-start | bytes 1622016 | tf_op jit(solution)/shard_map/all_gather | solution.py:418
  214.8 9.8 %all-to-all-start = ((s32[8,1,16]{2,1,0:T(1,128)}), s32[8,1,16]{2,1,0:T(1,128)S(1)}, u32[]{:S(2)}, u32[]{:S(2)}) async-start(s32[8,1,16]{2,1,0:T(1,128)} %bitcast.4), calls=%async_computation | async-start | bytes 8192 | tf_op jit(solution)/shard_map/all_to_all | solution.py:380
  224.6 11.1 %all-to-all-start.4 = ((bf16[8,16,704]{2,1,0:T(8,128)(2,1)}), bf16[8,16,704]{2,1,0:T(8,128)(2,1)S(1)}, u32[]{:S(2)}, u32[]{:S(2)}) async-start(bf16[8,16,704]{2,1,0:T(8,128)(2,1)} %bitcast.15), calls=%async_computation.4 | async-start | bytes 393216 | tf_op jit(solution)/shard_map/all_to_all | solution.py:380
  242.3 1.2 copy-start.1
Sparse Core Ops, SparseCore 0:
  10.4 66.9 all-gather.4
Sparse Core Ops, SparseCore 1:
  128.3 73.7 all-gather.8
  203.4 24.3 all-gather.6

commit v2 on v1

--- a/solution.py
+++ b/solution.py
@@ -331,6 +331,185 @@
             device_id={"tok": j},
             device_id_type=MESH,
         ).wait_recv()
+
+
+def merge_kernel(
+    n_tok,
+    heads_ref,
+    out_weight_ref,
+    patches_ref,
+    merger_ref,
+    slot_hit_ref,
+    row_hit_ref,
+    out_ref,
+    give,
+    got,
+    cut,
+    gathered,
+    totals,
+    parts,
+    packed,
+    arrived,
+    placed,
+    pair_sem,
+    cut_send,
+    cut_recv,
+    core_send,
+    core_recv,
+    part_send,
+    part_recv,
+    pack_send,
+    pack_recv,
+):
+    me, core = lax.axis_index("tok"), lax.axis_index("sub")
+    half, width = give.shape
+    quarter = half // 4
+    depth = merger_ref.shape[0]
+
+    barrier = pltpu.get_barrier_semaphore()
+    for d in range(1, n_tok):
+        pl.semaphore_signal(
+            barrier, inc=1, device_id={"tok": lax.rem(me + d, n_tok)}, device_id_type=MESH
+        )
+    pl.semaphore_signal(barrier, inc=1, device_id={"sub": 1 - core}, device_id_type=MESH)
+
+    def send(src, dst, send_sem, recv_sem, target):
+        return pltpu.make_async_remote_copy(
+            src_ref=src,
+            dst_ref=dst,
+            send_sem=send_sem,
+            recv_sem=recv_sem,
+            device_id=target,
+            device_id_type=MESH,
+        )
+
+    def projected(c):
+        total = jnp.zeros((half, width), jnp.float32)
+        for h in range(n_tok):
+            total = total + jnp.dot(
+                heads_ref[h, pl.ds(pl.multiple_of(c * half, half), half)],
+                out_weight_ref[h],
+                preferred_element_type=jnp.float32,
+            )
+        return total.astype(jnp.bfloat16)
+
+    sibling = {"sub": 1 - core}
+    give[...] = projected(1 - core)
+    pl.semaphore_wait(barrier, n_tok)
+    swap = send(give, got, pair_sem.at[0], pair_sem.at[1], sibling)
+    swap.start()
+    kept = projected(core)
+    swap.wait()
+    rows = patches_ref[pl.ds(pl.multiple_of(core * half, half), half)].astype(jnp.float32)
+    hidden = rows + (kept.astype(jnp.float32) + got[...].astype(jnp.float32))
+    merged = layer_norm(hidden).astype(jnp.bfloat16)
+    to_row = lax.broadcasted_iota(jnp.int32, (half, half), 0)
+    from_row = lax.broadcasted_iota(jnp.int32, (half, half), 1)
+    pick = jnp.where(
+        from_row == 4 * lax.rem(to_row, quarter) + lax.div(to_row, quarter), 1.0, 0.0
+    ).astype(jnp.bfloat16)
+    split = jnp.dot(pick, merged, preferred_element_type=jnp.float32).astype(jnp.bfloat16)
+    per_row = width // depth
+    for t in range(n_tok):
+        j, u = t // per_row, t % per_row
+        cut[t] = split[j * quarter : (j + 1) * quarter, u * depth : (u + 1) * depth]
+
+    def cut_copy(t, source):
+        return send(
+            cut.at[t], gathered.at[source, core], cut_send.at[t], cut_recv.at[source], {"tok": t}
+        )
+
+    def core_copy(t, c):
+        return send(
+            gathered.at[t, c], gathered.at[t, c], core_send.at[t], core_recv.at[t], sibling
+        )
+
+    def part_copy(t, source):
+        return send(totals.at[t], parts.at[source], part_send.at[t], part_recv.at[source], {"tok": t})
+
+    def pack_copy(t, source):
+        return send(packed.at[t], arrived.at[source], pack_send.at[t], pack_recv.at[source], {"tok": t})
+
+    others = [lax.rem(me + d, n_tok) for d in range(1, n_tok)]
+    backward = [lax.rem(me + n_tok - d, n_tok) for d in range(1, n_tok)]
+    for t in others:
+        cut_copy(t, me).start()
+    gathered[me, core] = cut[me]
+    core_copy(me, core).start()
+    for t in backward:
+        cut_copy(t, t).wait_recv()
+        core_copy(t, core).start()
+
+    def meet(t):
+        core_copy(t, 1 - core).wait_recv()
+        block = gathered[t].reshape(2 * quarter, depth)
+        return jnp.dot(block, merger_ref[...], preferred_element_type=jnp.float32).astype(jnp.bfloat16)
+
+    parts[me] = meet(me)
+    for t in backward:
+        totals[t] = meet(t)
+        part_copy(t, me).start()
+    total = parts[me].astype(jnp.float32)
+    for t in others:
+        part_copy(t, t).wait_recv()
+        total = total + parts[t].astype(jnp.float32)
+    sums = total.astype(jnp.bfloat16)
+    capacity = packed.shape[1]
+    slots = jnp.dot(slot_hit_ref[...], sums, preferred_element_type=jnp.float32).astype(jnp.bfloat16)
+    packed[...] = slots.reshape(n_tok, capacity, slots.shape[1])
+    for t in others:
+        pack_copy(t, me).start()
+    arrived[me] = packed[me]
+    for t in backward:
+        pack_copy(t, t).wait_recv()
+    tokens = arrived[...].reshape(n_tok * capacity, arrived.shape[2])
+    landed = jnp.dot(row_hit_ref[...], tokens, preferred_element_type=jnp.float32).astype(jnp.bfloat16)
+    placed[...] = landed.reshape(placed.shape)
+    last = send(placed.at[1 - core], out_ref.at[core], pair_sem.at[2], pair_sem.at[3], sibling)
+    last.start()
+    out_ref[core] = placed[core]
+    last.wait()
+    core_copy(me, core).wait_send()
+    for t in others:
+        cut_copy(t, me).wait_send()
+        core_copy(t, core).wait_send()
+        part_copy(t, me).wait_send()
+        pack_copy(t, me).wait_send()
+
+
+def merged_tokens(heads, out_weight, patches, merger_weight, slot_hit, row_hit, n_tok):
+    count, width = patches.shape
+    depth, narrow = merger_weight.shape
+    groups, capacity = count // 4, slot_hit.shape[0] // n_tok
+    piece_rows = row_hit.shape[0]
+    bf16 = jnp.bfloat16
+    vmem = pl.BlockSpec(memory_space=pltpu.VMEM)
+    each = pltpu.SemaphoreType.DMA((n_tok,))
+    return pl.pallas_call(
+        functools.partial(merge_kernel, n_tok),
+        out_shape=jax.ShapeDtypeStruct((2, piece_rows // 2, narrow), bf16),
+        in_specs=[vmem] * 6,
+        out_specs=vmem,
+        scratch_shapes=[
+            pltpu.VMEM((count // 2, width), bf16),
+            pltpu.VMEM((count // 2, width), bf16),
+            pltpu.VMEM((n_tok, groups // 2, depth), bf16),
+            pltpu.VMEM((n_tok, 2, groups // 2, depth), bf16),
+            pltpu.VMEM((n_tok, groups, narrow), bf16),
+            pltpu.VMEM((n_tok, groups, narrow), bf16),
+            pltpu.VMEM((n_tok, capacity, narrow), bf16),
+            pltpu.VMEM((n_tok, capacity, narrow), bf16),
+            pltpu.VMEM((2, piece_rows // 2, narrow), bf16),
+            pltpu.SemaphoreType.DMA((4,)),
+        ]
+        + [each] * 8,
+        compiler_params=pltpu.CompilerParams(
+            collective_id=2, has_side_effects=True, vmem_limit_bytes=40 * 1024 * 1024
+        ),
+        cost_estimate=pl.CostEstimate(
+            flops=2 * count * width * n_tok * LANES, bytes_accessed=8 * count * width, transcendentals=0
+        ),
+    )(heads, out_weight, patches, merger_weight, slot_hit, row_hit)
 
 
 def heads_of(kind, half_rows, weight, info, n_tok):
@@ -421,28 +600,6 @@
         lax.all_gather(decoder_outproj, ("grp", "tok"), axis=1, tiled=True), head_local
     )
 
-    image_ends = lax.all_gather(jnp.cumsum(image_sizes, axis=1), "tok", axis=0, tiled=True)
-    half_patches = lax.dynamic_slice_in_dim(patches, core * (patch_count // 2), patch_count // 2, 0)
-    heads = heads_of("image", half_patches, vision_weight, image_ends, n_tok)
-    partial_value = jnp.einsum("hrc,hcn->rn", heads, vision_out, preferred_element_type=f32).astype(
-        bf16
-    )
-    other = lax.ppermute(partial_value, "sub", [(0, 1), (1, 0)])
-    hidden = patches.astype(f32) + (partial_value.astype(f32) + other.astype(f32))
-    merged = layer_norm(hidden).astype(bf16)
-
-    group_count = patch_count // 4
-    shard_depth = merger_weight.shape[0]
-    parts = 4 * width // shard_depth
-    cut = merged.reshape(group_count, 4, parts // 4, shard_depth).transpose(1, 2, 0, 3)
-    gathered = across(cut.reshape(parts, group_count, shard_depth), "tok")
-    partial_embed = jnp.dot(
-        gathered.reshape(n_tok * group_count, shard_depth), merger_weight, preferred_element_type=f32
-    ).astype(bf16)
-    embedded = jnp.sum(
-        across(partial_embed.reshape(n_tok, group_count, half_width), "tok").astype(f32), axis=0
-    ).astype(bf16)
-
     capacity = patch_count // (2 * n_tok)
     targets = image_positions[0]
     target_chip = targets // piece_rows
@@ -452,14 +609,20 @@
     slot = target_chip * capacity + slot_index
     slot_hit = jnp.arange(n_tok * capacity, dtype=jnp.int32)[:, None] == slot[None, :]
     row_buffer = jnp.sum(jnp.where(slot_hit, target_row[None, :] + 1, 0), axis=1) - 1
-    arrived_rows = across(row_buffer.reshape(n_tok, capacity), "tok").reshape(-1)
-    packed = jnp.dot(slot_hit.astype(bf16), embedded, preferred_element_type=f32).astype(bf16)
-    narrow_rows = across(packed.reshape(n_tok, capacity, half_width), "tok").reshape(-1, half_width)
+    own_ends = jnp.broadcast_to(jnp.cumsum(image_sizes, axis=1), (n_tok, image_sizes.shape[1]))
+    numbers = across(
+        jnp.concatenate([row_buffer.reshape(n_tok, capacity), own_ends], axis=1), "tok"
+    )
+    arrived_rows, image_ends = numbers[:, :capacity].reshape(-1), numbers[:, capacity:]
     row_hit = jnp.arange(piece_rows, dtype=jnp.int32)[:, None] == arrived_rows[None, :]
-    placed = jnp.dot(row_hit.astype(bf16), narrow_rows, preferred_element_type=f32).astype(bf16)
+
+    half_patches = lax.dynamic_slice_in_dim(patches, core * (patch_count // 2), patch_count // 2, 0)
+    heads = heads_of("image", half_patches, vision_weight, image_ends, n_tok)
+    halves = merged_tokens(
+        heads, vision_out, patches, merger_weight, slot_hit.astype(bf16), row_hit.astype(bf16), n_tok
+    )
     half_piece = piece_rows // 2
-    swapped = across(placed.reshape(2, half_piece, half_width), "sub")
-    image_rows = swapped.transpose(1, 0, 2).reshape(half_piece, width)
+    image_rows = halves.transpose(1, 0, 2).reshape(half_piece, width)
     filled = lax.dynamic_slice_in_dim(
         jnp.any(row_hit, axis=1).astype(jnp.int32), core * half_piece, half_piece, 0
     )

time: 289 us -> 260 us (0.90)
  Pallas kernels: 90.5 us -> 147 us
  waiting for transfers between devices: 70.4 us -> 34.6 us
  starting transfers between devices: 27.9 us -> 7.61 us
  blocking collectives: 49 us -> 35.6 us
  local copies, waits for them, and re-layouts: 25.2 us -> 18.6 us
  matrix products: 4.5 us -> 0.57 us
  other arithmetic: 5.8 us -> 2.54 us
    pallas_call x0 -> x1, Pallas kernels: none -> 57.2 us  [merged_tokens(): pl.pallas_call(functools.partial(merge_kernel, n_tok), out_shape=jax.Shap...]
    all_gather x1 -> x0, blocking collectives: 40.6 us -> none  [shards(): lax.all_gather(jnp.cumsum(image_sizes, axis=1), 'tok', axis=0, tiled=True)]
    all_to_all x6 -> x2, waiting for transfers between devices: 67.8 us -> 33.2 us  [across(): return lax.all_to_all(block, axis, split_axis=0, concat_axis=0, tiled=True)]
    all_to_all x2, blocking collectives: 8.34 us -> 35.6 us  [across(): return lax.all_to_all(block, axis, split_axis=0, concat_axis=0, tiled=True)]
    all_to_all x6 -> x2, starting transfers between devices: 27.5 us -> 7.53 us  [across(): return lax.all_to_all(block, axis, split_axis=0, concat_axis=0, tiled=True)]
    dot_general x4 -> x0, matrix products: 3.91 us -> none  [the longest x1 2.6 us: shards(): jnp.einsum('hrc,hcn->rn', heads, vision_out, preferred_element_type=f32)]
    reshape x2 -> x1, local copies, waits for them, and re-layouts: 3.48 us -> 0.18 us  [shards(): image_rows = halves.transpose(1, 0, 2).reshape(half_piece, width)]
  transfers between devices with their start and end apart: 10 -> 5, of which waited for: 6 -> 2; matrix products, arithmetic and copies ran while one was open for 9% -> 6% of each run, Pallas kernels for 20% -> 57%
where the time goes in v2:
time: 260 us
  Pallas kernels  147 us (57%)
  blocking collectives  35.6 us (14%)
  waiting for transfers between devices  34.6 us (13%)
  local copies, waits for them, and re-layouts  18.6 us (7%)
  between operations  13.4 us (5%)
  starting transfers between devices  7.61 us (3%)
    pallas_call x2, Pallas kernels, heads_of(): pl.pallas_call(functools.partial(head_kernel, kind, n_tok), out_shape=jax...  89.5 us
    pallas_call x1, Pallas kernels, merged_tokens(): pl.pallas_call(functools.partial(merge_kernel, n_tok), out_shape=jax.Shap...  57.2 us
    all_to_all x2, blocking collectives, across(): return lax.all_to_all(block, axis, split_axis=0, concat_axis=0, tiled=True)  35.6 us
    all_to_all x2, waiting for transfers between devices, across(): return lax.all_to_all(block, axis, split_axis=0, concat_axis=0, tiled=True)  33.2 us
    all_to_all x2, starting transfers between devices, across(): return lax.all_to_all(block, axis, split_axis=0, concat_axis=0, tiled=True)  7.53 us
  transfers between devices with their start and end apart: 5, of which 2 were waited for; matrix products, arithmetic and copies ran while one was open for 6% of the time, Pallas kernels for 57%

profile of v2, /device:TPU:0, one launch (start us, length us, event | category | flops | bytes accessed | tf_op | source)
XLA Modules:
  0.0 259.7 jit_solution(1414699388367067414)
XLA Ops:
  6.5 0.7 all-gather.4.cloned.1.call-update
  7.3 1.7 reshape.94
  9.0 0.5 copy.30
  10.3 31.6 %all_to_all.27 = bf16[8,88,384]{2,1,0:T(8,128)(2,1)} all-to-all(bf16[8,88,384]{2,1,0:T(8,128)(2,1)S(1)} %reshape.95), channel_id=1, replica_groups=mesh['grp'=2,'tok'=8,'sub'=2] {'tok'}, dimensions={0} | all-to-all | bytes 1081344 | tf_op jit(solution)/shard_map/all_to_all | solution.py:559
  42.0 0.7 all-gather.8.cloned.1.call-update
  43.5 0.6 pad_add_fusion
  44.1 3.3 %all-to-all-start = ((s32[8,1,20]{2,1,0:T(1,128)}), s32[8,1,20]{2,1,0:T(1,128)S(1)}, u32[]{:S(2)}, u32[]{:S(2)}) async-start(s32[8,1,20]{2,1,0:T(1,128)} %bitcast.7), calls=%async_computation | async-start | bytes 8192 | tf_op jit(solution)/shard_map/all_to_all | solution.py:559
  47.5 1.2 reshape.89
  48.6 0.9 copy.29
  49.6 0.8 pad.15
  50.4 1.7 reshape.90
  52.1 1.7 all-to-all-done
  53.8 4.2 %all-to-all-start.1 = ((bf16[8,176,384]{2,1,0:T(8,128)(2,1)}), bf16[8,176,384]{2,1,0:T(8,128)(2,1)S(1)}, u32[]{:S(2)}, u32[]{:S(2)}) async-start(bf16[8,176,384]{2,1,0:T(8,128)(2,1)} %reshape.90), calls=%async_computation.1 | async-start | bytes 2162688 | tf_op jit(solution)/shard_map/all_to_all | solution.py:559
  58.7 31.4 %all-to-all-done.1 = bf16[8,176,384]{2,1,0:T(8,128)(2,1)S(1)} async-done(((bf16[8,176,384]{2,1,0:T(8,128)(2,1)}), bf16[8,176,384]{2,1,0:T(8,128)(2,1)S(1)}, u32[]{:S(2)}, u32[]{:S(2)}) %all-to-all-start.1) | async-done | bytes 1081376 | tf_op jit(solution)/shard_map/all_to_all | solution.py:559
  90.1 52.7 %shard_map.100.heads_ref = bf16[8,256,128]{2,1,0:T(8,128)(2,1)S(1)} custom-call(bf16[128,1408]{1,0:T(8,128)(2,1)S(1)} %constant_dynamic-slice_fusion.x_ref, bf16[1408,384]{1,0:T(8,128)(2,1)S(1)} %bitcast.48, s32[8,4]{1,0:T(8,128)S(1)} %slice.7.info_ref), custom_call_target="tpu_custom_call" | custom-call | flops 2214592512 | bytes 5767168 | tf_op jit(solution)/shard_map/pallas_call | solution.py:521
  142.8 4.1 %copy.23 = bf16[704,1408]{1,0:T(8,128)(2,1)} copy(bf16[704,1408]{0,1:T(8,128)(2,1)} %all-gather.4.cloned.1.call-done) | data formatting | bytes 3964928 | tf_op jit(solution)/shard_map/all_gather | solution.py:598
  147.0 1.9 pad.16.out_weight_ref
  148.9 57.2 %shard_map.101 = bf16[2,64,704]{2,1,0:T(8,128)(2,1)S(1)} custom-call(bf16[8,256,128]{2,1,0:T(8,128)(2,1)S(1)} %shard_map.100.heads_ref, bf16[8,128,1408]{2,1,0:T(8,128)(2,1)S(1)} %pad.16.out_weight_ref, bf16[256,1408]{1,0:T(8,128)(2,1)S(1)} %copy-done, bf16[704,704]{1,0:T(8,128)(2,1)S(1)} %copy-done.1, bf16[128,64]{1,0:T(8,128)(2,1)S(1)} %fusion.8.slot_hit_ref, ...), custom_call_target="tpu_custom_call" | custom-call | flops 738197504 | bytes 2883584 | tf_op jit(solution)/shard_map/pallas_call | solution.py:488
  206.6 1.2 copy-done.2
  207.9 36.9 %shard_map.102 = bf16[8,128,128]{2,1,0:T(8,128)(2,1)S(1)} custom-call(bf16[64,1408]{1,0:T(8,128)(2,1)S(1)} %dynamic-slice_select_fusion.x_ref, bf16[1408,384]{1,0:T(8,128)(2,1)S(1)} %copy-done.2, s32[1,2]{1,0:T(1,128)S(1)} %sub.25.info_ref), custom_call_target="tpu_custom_call" | custom-call | flops 1107296256 | bytes 2883584 | tf_op jit(solution)/shard_map/pallas_call | solution.py:521
  244.7 3.1 %copy.26 = bf16[704,1408]{1,0:T(8,128)(2,1)S(1)} copy(bf16[704,1408]{0,1:T(8,128)(2,1)} %all-gather.8.cloned.1.call-done) | data formatting | bytes 3964928 | tf_op jit(solution)/shard_map/all_gather | solution.py:600
  247.9 0.6 fusion.5
  248.4 4.0 %all_to_all.28 = bf16[2,64,1408]{2,1,0:T(8,128)(2,1)S(1)} all-to-all(bf16[2,64,1408]{2,1,0:T(8,128)(2,1)S(1)} %bitcast.55), channel_id=1, replica_groups=mesh['grp'=2,'tok'=8,'sub'=2] {'sub'}, dimensions={0} | all-to-all | bytes 720896 | tf_op jit(solution)/shard_map/all_to_all | solution.py:559
  252.4 0.8 reduce_sum.35
  (46 shorter events, 3.0 us)
Async XLA Ops:
  6.5 136.3 %all-gather.4.cloned.1.call-start = ((), (), s32[]{:S(2)}) async-start(), calls=%async_computation.4 | async-start | bytes 2433024 | tf_op jit(solution)/shard_map/all_gather | solution.py:598
  7.3 199.4 %all-gather.6.cloned.1.call-start = ((), (), s32[]{:S(2)}) async-start(), calls=%async_computation.5 | async-start | bytes 1622016 | tf_op jit(solution)/shard_map/all_gather | solution.py:597
  9.4 33.2 %copy-start.5 = (s32[1,64]{1,0:T(1,128)S(1)}, s32[1,64]{1,0:T(1,128)}, u32[]{:S(2)}) copy-start(s32[1,64]{1,0:T(1,128)} %param.16) | copy-start | bytes 772
  9.5 33.8 %copy-start.6 = (s32[1,4]{1,0:T(1,128)S(1)}, s32[1,4]{1,0:T(1,128)}, u32[]{:S(2)}) copy-start(s32[1,4]{1,0:T(1,128)} %param.11) | copy-start | bytes 52
  9.5 38.0 %copy-start.3 = (bf16[176,1,3,704]{3,0,2,1:T(8,128)(2,1)S(1)}, bf16[176,1,3,704]{3,0,2,1:T(8,128)(2,1)}, u32[]{:S(2)}) copy-start(bf16[176,1,3,704]{3,0,2,1:T(8,128)(2,1)} %param.12) | copy-start | bytes 2230276
  41.9 202.8 %all-gather.8.cloned.1.call-start = ((), (), s32[]{:S(2)}) async-start(), calls=%async_computation.6 | async-start | bytes 2297856 | tf_op jit(solution)/shard_map/all_gather | solution.py:600
  44.1 9.7 %all-to-all-start = ((s32[8,1,20]{2,1,0:T(1,128)}), s32[8,1,20]{2,1,0:T(1,128)S(1)}, u32[]{:S(2)}, u32[]{:S(2)}) async-start(s32[8,1,20]{2,1,0:T(1,128)} %bitcast.7), calls=%async_computation | async-start | bytes 8192 | tf_op jit(solution)/shard_map/all_to_all | solution.py:559
  50.3 7.7 %copy-start.7 = (s32[1,2]{1,0:T(1,128)S(1)}, s32[1,2]{1,0:T(1,128)}, u32[]{:S(2)}) copy-start(s32[1,2]{1,0:T(1,128)} %param.17) | copy-start | bytes 28
  50.4 7.9 %copy-start = (bf16[256,1408]{1,0:T(8,128)(2,1)S(1)}, bf16[256,1408]{1,0:T(8,128)(2,1)}, u32[]{:S(2)}) copy-start(bf16[256,1408]{1,0:T(8,128)(2,1)} %patches_ref.1) | copy-start | bytes 2162692
  53.8 36.3 %all-to-all-start.1 = ((bf16[8,176,384]{2,1,0:T(8,128)(2,1)}), bf16[8,176,384]{2,1,0:T(8,128)(2,1)S(1)}, u32[]{:S(2)}, u32[]{:S(2)}) async-start(bf16[8,176,384]{2,1,0:T(8,128)(2,1)} %reshape.90), calls=%async_computation.1 | async-start | bytes 2162688 | tf_op jit(solution)/shard_map/all_to_all | solution.py:559
  147.0 1.9 copy-start.1
  148.8 57.6 %copy-start.4 = (bf16[128,1408]{1,0:T(8,128)(2,1)S(1)}, bf16[128,1408]{1,0:T(8,128)(2,1)}, u32[]{:S(2)}) copy-start(bf16[128,1408]{1,0:T(8,128)(2,1)} %param.15) | copy-start | bytes 1081348
  206.6 1.2 copy-start.2
Sparse Core Ops, SparseCore 0:
  9.5 66.6 all-gather.3
  77.8 23.9 all-gather.5
  104.5 72.3 all-gather.7

commit v3 on v2

--- a/solution.py
+++ b/solution.py
@@ -156,9 +156,22 @@
 
 
 def head_kernel(
-    kind, n_tok, x_ref, w_ref, info_ref, out_ref, buf, staged, kv, send_sem, recv_sem, back_send, back_recv
+    kind,
+    n_tok,
+    x_ref,
+    weight_ref,
+    info_ref,
+    *rest,
 ):
-    me, core = lax.axis_index("tok"), lax.axis_index("sub")
+    if kind == "image":
+        out_ref, buf, staged, kv, send_sem, recv_sem, back_send, back_recv, *own_scratch = rest
+        w_ref, w_send, w_recv, w_pass = own_scratch
+        mixed = out_ref
+    else:
+        last_weight_ref, out_ref, buf, staged, kv, send_sem, recv_sem, back_send, back_recv, *own_scratch = rest
+        mixed, give, got, pair_sem = own_scratch
+        w_ref = weight_ref
+    me, core, grp = lax.axis_index("tok"), lax.axis_index("sub"), lax.axis_index("grp")
     rows = 2 * x_ref.shape[0]
     z, y = lax.div(me, 2), lax.rem(me, 2)
     n_z = n_tok // 2
@@ -171,9 +184,14 @@
         )
     pl.semaphore_signal(barrier, inc=1, device_id={"sub": 1 - core}, device_id_type=MESH)
 
+    greeted = n_tok
+    if kind == "image":
+        pl.semaphore_signal(barrier, inc=1, device_id={"grp": 1 - grp}, device_id_type=MESH)
+        greeted = n_tok + 1
+        w_ref[me] = weight_ref[me]
     own = x_ref[...].astype(jnp.float32)
     buf[me, core] = layer_norm(own).astype(jnp.bfloat16)
-    pl.semaphore_wait(barrier, n_tok)
+    pl.semaphore_wait(barrier, greeted)
 
     def push(t, way):
         target = [{"tok": me + 2}, {"tok": me - 2}, {"tok": side}, {"sub": 1 - core}][way]
@@ -244,13 +262,57 @@
                     wait(side + 2 * k - 2)
                     act(side + 2 * k - 2, 3)
 
+    def weight_copy(t, source):
+        return pltpu.make_async_remote_copy(
+            src_ref=weight_ref.at[t],
+            dst_ref=w_ref.at[source],
+            send_sem=w_send.at[t],
+            recv_sem=w_recv.at[source],
+            device_id={"tok": t},
+            device_id_type=MESH,
+        )
+
+    def weight_pass(t):
+        return pltpu.make_async_remote_copy(
+            src_ref=w_ref.at[t],
+            dst_ref=w_ref.at[t],
+            send_sem=w_pass.at[t],
+            recv_sem=w_recv.at[t],
+            device_id={"grp": 1 - grp},
+            device_id_type=MESH,
+        )
+
+    others = [lax.rem(me + d, n_tok) for d in range(1, n_tok)]
+
+    def mine(t):
+        return lax.rem(lax.div(t, 2), 2) == grp
+
+    if kind == "image":
+        @pl.when(mine(me))
+        def _():
+            for t in others:
+                weight_copy(t, me).start()
+
     run(lambda t, way: push(t, way).start(), lambda t: arrived(t, core))
+    if kind == "image":
+        for t in others:
+            @pl.when(mine(t))
+            def _():
+                weight_copy(t, t).wait_recv()
+                weight_pass(t).start()
+
+        for t in others:
+            @pl.when(jnp.logical_not(mine(t)))
+            def _():
+                weight_pass(t).wait_recv()
+
     for t in range(n_tok):
         arrived(t, 1 - core)
 
     def project(j):
         block = buf[j].reshape(rows, buf.shape[3])
-        return jnp.dot(block, w_ref[...], preferred_element_type=jnp.float32).astype(jnp.bfloat16)
+        weight = w_ref[...].reshape(buf.shape[3], 3 * LANES)
+        return jnp.dot(block, weight, preferred_element_type=jnp.float32).astype(jnp.bfloat16)
 
     def mix(query, key, value, allowed):
         scores = lax.dot_general(
@@ -263,7 +325,7 @@
     def back(j):
         return pltpu.make_async_remote_copy(
             src_ref=staged.at[j],
-            dst_ref=out_ref.at[me],
+            dst_ref=mixed.at[me],
             send_sem=back_send.at[j],
             recv_sem=back_recv.at[me],
             device_id={"tok": j},
@@ -313,7 +375,7 @@
 
         @pl.when(d == n_tok)
         def _():
-            out_ref[me] = mixture
+            mixed[me] = mixture
 
         return carry
 
@@ -325,12 +387,115 @@
         back(j).wait_send()
         pltpu.make_async_remote_copy(
             src_ref=staged.at[j],
-            dst_ref=out_ref.at[j],
+            dst_ref=mixed.at[j],
             send_sem=back_send.at[j],
             recv_sem=back_recv.at[j],
             device_id={"tok": j},
             device_id_type=MESH,
         ).wait_recv()
+    if kind == "image":
+        @pl.when(mine(me))
+        def _():
+            for t in others:
+                weight_copy(t, me).wait_send()
+
+        for t in others:
+            @pl.when(mine(t))
+            def _():
+                weight_pass(t).wait_send()
+
+        return
+
+    half = rows // 2
+
+    def projected(c):
+        total = jnp.zeros((half, out_ref.shape[1]), jnp.float32)
+        for h in range(n_tok):
+            total = total + lax.dot_general(
+                mixed[h, pl.ds(pl.multiple_of(c * half, half), half)],
+                last_weight_ref[:, h * LANES : (h + 1) * LANES],
+                (((1,), (1,)), ((), ())),
+                preferred_element_type=jnp.float32,
+            )
+        return total.astype(jnp.bfloat16)
+
+    give[...] = projected(1 - core)
+    swap = pltpu.make_async_remote_copy(
+        src_ref=give,
+        dst_ref=got,
+        send_sem=pair_sem.at[0],
+        recv_sem=pair_sem.at[1],
+        device_id={"sub": 1 - core},
+        device_id_type=MESH,
+    )
+    swap.start()
+    kept = projected(core)
+    swap.wait()
+    out_ref[...] = (kept.astype(jnp.float32) + got[...].astype(jnp.float32)).astype(jnp.bfloat16)
+
+
+def heads_of(kind, half_rows, weight, info, n_tok, last_weight=None):
+    half, width = half_rows.shape
+    rows = 2 * half
+    bf16 = jnp.bfloat16
+    vmem = pl.BlockSpec(memory_space=pltpu.VMEM)
+    total = n_tok * rows
+    each = pltpu.SemaphoreType.DMA((n_tok,))
+    mixed = (n_tok, rows, LANES)
+    operands = [half_rows, weight, info]
+    if kind == "image":
+        out_shape, kv_shape = mixed, (1, 16, LANES)
+        extra = [pltpu.VMEM(weight.shape, bf16), each, each, each]
+    else:
+        out_shape, kv_shape = (half, width), (n_tok + REACH, rows, 3 * LANES)
+        operands.append(last_weight)
+        extra = [
+            pltpu.VMEM(mixed, bf16),
+            pltpu.VMEM((half, width), bf16),
+            pltpu.VMEM((half, width), bf16),
+            pltpu.SemaphoreType.DMA((2,)),
+        ]
+    return pl.pallas_call(
+        functools.partial(head_kernel, kind, n_tok),
+        out_shape=jax.ShapeDtypeStruct(out_shape, bf16),
+        in_specs=[vmem, vmem, pl.BlockSpec(memory_space=pltpu.SMEM)] + [vmem] * (len(operands) - 3),
+        out_specs=vmem,
+        scratch_shapes=[
+            pltpu.VMEM((n_tok, 2, half, width), bf16),
+            pltpu.VMEM(mixed, bf16),
+            pltpu.VMEM(kv_shape, bf16),
+            pltpu.SemaphoreType.DMA((4, n_tok)),
+            pltpu.SemaphoreType.DMA((n_tok, 2)),
+            each,
+            each,
+        ]
+        + extra,
+        compiler_params=pltpu.CompilerParams(
+            collective_id=0 if kind == "image" else 1,
+            has_side_effects=True,
+            vmem_limit_bytes=40 * 1024 * 1024,
+        ),
+        cost_estimate=pl.CostEstimate(
+            flops=2 * total * width * 3 * LANES, bytes_accessed=2 * total * width, transcendentals=0
+        ),
+    )(*operands)
+
+
+def head_columns(weight, head_local):
+    rows = weight.shape[0]
+    split = weight.reshape(rows, 3, head_local, HD).transpose(2, 0, 1, 3)
+    split = jnp.pad(split, ((0, 0), (0, 0), (0, 0), (0, LANES - HD)))
+    return split.reshape(head_local, rows, 3 * LANES)
+
+
+def turned(weight, head_local):
+    split = weight.T.reshape(weight.shape[1], head_local, HD)
+    split = jnp.pad(split, ((0, 0), (0, 0), (0, LANES - HD)))
+    return split.reshape(weight.shape[1], head_local * LANES)
+
+
+def across(block, axis):
+    return lax.all_to_all(block, axis, split_axis=0, concat_axis=0, tiled=True)
 
 
 def merge_kernel(
@@ -341,7 +506,9 @@
     merger_ref,
     slot_hit_ref,
     row_hit_ref,
+    text_weight_ref,
     out_ref,
+    text_out_ref,
     give,
     got,
     cut,
@@ -360,8 +527,11 @@
     part_recv,
     pack_send,
     pack_recv,
+    text_send,
+    text_recv,
+    text_pass,
 ):
-    me, core = lax.axis_index("tok"), lax.axis_index("sub")
+    me, core, grp = lax.axis_index("tok"), lax.axis_index("sub"), lax.axis_index("grp")
     half, width = give.shape
     quarter = half // 4
     depth = merger_ref.shape[0]
@@ -372,6 +542,7 @@
             barrier, inc=1, device_id={"tok": lax.rem(me + d, n_tok)}, device_id_type=MESH
         )
     pl.semaphore_signal(barrier, inc=1, device_id={"sub": 1 - core}, device_id_type=MESH)
+    pl.semaphore_signal(barrier, inc=1, device_id={"grp": 1 - grp}, device_id_type=MESH)
 
     def send(src, dst, send_sem, recv_sem, target):
         return pltpu.make_async_remote_copy(
@@ -386,16 +557,42 @@
     def projected(c):
         total = jnp.zeros((half, width), jnp.float32)
         for h in range(n_tok):
-            total = total + jnp.dot(
+            total = total + lax.dot_general(
                 heads_ref[h, pl.ds(pl.multiple_of(c * half, half), half)],
-                out_weight_ref[h],
+                out_weight_ref[:, h * LANES : (h + 1) * LANES],
+                (((1,), (1,)), ((), ())),
                 preferred_element_type=jnp.float32,
             )
         return total.astype(jnp.bfloat16)
 
     sibling = {"sub": 1 - core}
+    def text_copy(t, source):
+        return send(
+            text_weight_ref.at[t],
+            text_out_ref.at[grp * n_tok + source],
+            text_send.at[t],
+            text_recv.at[grp * n_tok + source],
+            {"tok": t},
+        )
+
+    def text_forward(t, g):
+        slot = g * n_tok + t
+        return send(
+            text_out_ref.at[slot],
+            text_out_ref.at[slot],
+            text_pass.at[t],
+            text_recv.at[slot],
+            {"grp": 1 - grp},
+        )
+
+    others = [lax.rem(me + d, n_tok) for d in range(1, n_tok)]
+    backward = [lax.rem(me + n_tok - d, n_tok) for d in range(1, n_tok)]
+    text_out_ref[grp * n_tok + me] = text_weight_ref[me]
+    pl.semaphore_wait(barrier, n_tok + 1)
+    for t in others:
+        text_copy(t, me).start()
+    text_forward(me, grp).start()
     give[...] = projected(1 - core)
-    pl.semaphore_wait(barrier, n_tok)
     swap = send(give, got, pair_sem.at[0], pair_sem.at[1], sibling)
     swap.start()
     kept = projected(core)
@@ -430,8 +627,6 @@
     def pack_copy(t, source):
         return send(packed.at[t], arrived.at[source], pack_send.at[t], pack_recv.at[source], {"tok": t})
 
-    others = [lax.rem(me + d, n_tok) for d in range(1, n_tok)]
-    backward = [lax.rem(me + n_tok - d, n_tok) for d in range(1, n_tok)]
     for t in others:
         cut_copy(t, me).start()
     gathered[me, core] = cut[me]
@@ -445,6 +640,9 @@
         block = gathered[t].reshape(2 * quarter, depth)
         return jnp.dot(block, merger_ref[...], preferred_element_type=jnp.float32).astype(jnp.bfloat16)
 
+    for t in backward:
+        text_copy(t, t).wait_recv()
+        text_forward(t, grp).start()
     parts[me] = meet(me)
     for t in backward:
         totals[t] = meet(t)
@@ -470,6 +668,12 @@
     out_ref[core] = placed[core]
     last.wait()
     core_copy(me, core).wait_send()
+    text_forward(me, grp).wait_send()
+    text_forward(me, 1 - grp).wait_recv()
+    for t in others:
+        text_copy(t, me).wait_send()
+        text_forward(t, grp).wait_send()
+        text_forward(t, 1 - grp).wait_recv()
     for t in others:
         cut_copy(t, me).wait_send()
         core_copy(t, core).wait_send()
@@ -477,7 +681,7 @@
         pack_copy(t, me).wait_send()
 
 
-def merged_tokens(heads, out_weight, patches, merger_weight, slot_hit, row_hit, n_tok):
+def merged_tokens(heads, out_weight, patches, merger_weight, slot_hit, row_hit, text_blocks, n_tok):
     count, width = patches.shape
     depth, narrow = merger_weight.shape
     groups, capacity = count // 4, slot_hit.shape[0] // n_tok
@@ -487,9 +691,12 @@
     each = pltpu.SemaphoreType.DMA((n_tok,))
     return pl.pallas_call(
         functools.partial(merge_kernel, n_tok),
-        out_shape=jax.ShapeDtypeStruct((2, piece_rows // 2, narrow), bf16),
-        in_specs=[vmem] * 6,
-        out_specs=vmem,
+        out_shape=(
+            jax.ShapeDtypeStruct((2, piece_rows // 2, narrow), bf16),
+            jax.ShapeDtypeStruct((2 * n_tok,) + text_blocks.shape[1:], bf16),
+        ),
+        in_specs=[vmem] * 7,
+        out_specs=(vmem, vmem),
         scratch_shapes=[
             pltpu.VMEM((count // 2, width), bf16),
             pltpu.VMEM((count // 2, width), bf16),
@@ -502,61 +709,15 @@
             pltpu.VMEM((2, piece_rows // 2, narrow), bf16),
             pltpu.SemaphoreType.DMA((4,)),
         ]
-        + [each] * 8,
+        + [each] * 9
+        + [pltpu.SemaphoreType.DMA((2 * n_tok,)), each],
         compiler_params=pltpu.CompilerParams(
             collective_id=2, has_side_effects=True, vmem_limit_bytes=40 * 1024 * 1024
         ),
         cost_estimate=pl.CostEstimate(
             flops=2 * count * width * n_tok * LANES, bytes_accessed=8 * count * width, transcendentals=0
         ),
-    )(heads, out_weight, patches, merger_weight, slot_hit, row_hit)
-
-
-def heads_of(kind, half_rows, weight, info, n_tok):
-    half, width = half_rows.shape
-    rows = 2 * half
-    kv_shape = (n_tok + REACH, rows, 3 * LANES) if kind == "text" else (1, 16, LANES)
-    vmem = pl.BlockSpec(memory_space=pltpu.VMEM)
-    total = n_tok * rows
-    return pl.pallas_call(
-        functools.partial(head_kernel, kind, n_tok),
-        out_shape=jax.ShapeDtypeStruct((n_tok, rows, LANES), jnp.bfloat16),
-        in_specs=[vmem, vmem, pl.BlockSpec(memory_space=pltpu.SMEM)],
-        out_specs=vmem,
-        scratch_shapes=[
-            pltpu.VMEM((n_tok, 2, half, width), jnp.bfloat16),
-            pltpu.VMEM((n_tok, rows, LANES), jnp.bfloat16),
-            pltpu.VMEM(kv_shape, jnp.bfloat16),
-            pltpu.SemaphoreType.DMA((4, n_tok)),
-            pltpu.SemaphoreType.DMA((n_tok, 2)),
-            pltpu.SemaphoreType.DMA((n_tok,)),
-            pltpu.SemaphoreType.DMA((n_tok,)),
-        ],
-        compiler_params=pltpu.CompilerParams(
-            collective_id=0 if kind == "image" else 1,
-            has_side_effects=True,
-            vmem_limit_bytes=40 * 1024 * 1024,
-        ),
-        cost_estimate=pl.CostEstimate(
-            flops=2 * total * width * 3 * LANES, bytes_accessed=2 * total * width, transcendentals=0
-        ),
-    )(half_rows, weight, info)
-
-
-def head_columns(weight, head_local):
-    rows = weight.shape[0]
-    split = weight.reshape(rows, 3, head_local, HD).transpose(2, 0, 1, 3)
-    split = jnp.pad(split, ((0, 0), (0, 0), (0, 0), (0, LANES - HD)))
-    return split.reshape(head_local, rows, 3 * LANES)
-
-
-def head_rows(weight, head_local):
-    split = weight.reshape(head_local, HD, weight.shape[1])
-    return jnp.pad(split, ((0, 0), (0, LANES - HD), (0, 0)))
-
-
-def across(block, axis):
-    return lax.all_to_all(block, axis, split_axis=0, concat_axis=0, tiled=True)
+    )(heads, out_weight, patches, merger_weight, slot_hit, row_hit, text_blocks)
 
 
 def shards(
@@ -574,7 +735,7 @@
     n_tok = lax.axis_size("tok")
     half_width = vision_inproj.shape[3]
     head_local = half_width // HD
-    if n_tok != head_local or lax.axis_size("sub") != 2:
+    if n_tok != head_local or lax.axis_size("sub") != 2 or lax.axis_size("grp") != 2:
         return shards_general(
             patches,
             image_sizes,
@@ -590,15 +751,13 @@
     core = lax.axis_index("sub")
     patch_count, width = patches.shape
     piece_rows = text_embed.shape[0]
-    bf16, f32 = jnp.bfloat16, jnp.float32
-
-    vision_weight = across(head_columns(vision_inproj, head_local), "tok").reshape(width, 3 * LANES)
-    text_part = across(head_columns(decoder_inproj, head_local), "tok").reshape(-1, 3 * LANES)
-    text_weight = lax.all_gather(text_part, "grp", axis=0, tiled=True)
-    vision_out = head_rows(lax.all_gather(vision_outproj, "tok", axis=1, tiled=True), head_local)
-    text_out = head_rows(
-        lax.all_gather(decoder_outproj, ("grp", "tok"), axis=1, tiled=True), head_local
-    )
+    bf16 = jnp.bfloat16
+
+    vision_blocks = head_columns(vision_inproj, head_local)
+    text_depth = decoder_inproj.shape[0]
+    text_blocks = jnp.pad(head_columns(decoder_inproj, head_local), ((0, 0), (0, -text_depth % 16), (0, 0)))
+    vision_out = lax.all_gather(turned(vision_outproj, head_local), "tok", axis=0, tiled=True)
+    text_out = lax.all_gather(turned(decoder_outproj, head_local), ("grp", "tok"), axis=0, tiled=True)
 
     capacity = patch_count // (2 * n_tok)
     targets = image_positions[0]
@@ -617,10 +776,18 @@
     row_hit = jnp.arange(piece_rows, dtype=jnp.int32)[:, None] == arrived_rows[None, :]
 
     half_patches = lax.dynamic_slice_in_dim(patches, core * (patch_count // 2), patch_count // 2, 0)
-    heads = heads_of("image", half_patches, vision_weight, image_ends, n_tok)
-    halves = merged_tokens(
-        heads, vision_out, patches, merger_weight, slot_hit.astype(bf16), row_hit.astype(bf16), n_tok
-    )
+    heads = heads_of("image", half_patches, vision_blocks, image_ends, n_tok)
+    halves, text_parts = merged_tokens(
+        heads,
+        vision_out,
+        patches,
+        merger_weight,
+        slot_hit.astype(bf16),
+        row_hit.astype(bf16),
+        text_blocks,
+        n_tok,
+    )
+    text_weight = text_parts[:, :text_depth].reshape(width, 3 * LANES)
     half_piece = piece_rows // 2
     image_rows = halves.transpose(1, 0, 2).reshape(half_piece, width)
     filled = lax.dynamic_slice_in_dim(
@@ -630,10 +797,7 @@
     decoder_input = jnp.where(filled[:, None] > 0, image_rows, text_half)
 
     starts = jnp.cumsum(prompt_lengths, axis=1) - prompt_lengths
-    text_heads = heads_of("text", decoder_input, text_weight, starts, n_tok)
-    text_partial = jnp.einsum("hrc,hcn->rn", text_heads, text_out, preferred_element_type=f32)
-    pair = across(text_partial.astype(bf16).reshape(2, half_piece, width), "sub")
-    return jnp.sum(pair.astype(f32), axis=0).astype(bf16)
+    return heads_of("text", decoder_input, text_weight, starts, n_tok, text_out)
 
 
 def solution(mesh):

time: 260 us -> 262 us (level)
  Pallas kernels: 147 us -> 218 us
  blocking collectives: 35.6 us -> 0 us
  waiting for transfers between devices: 34.6 us -> 0.06 us
    pallas_call x2, Pallas kernels: 89.5 us -> 150 us  [heads_of(): pl.pallas_call(functools.partial(head_kernel, kind, n_tok), out_shape=jax...]
    all_to_all x2 -> x0, blocking collectives: 35.6 us -> none  [across(): return lax.all_to_all(block, axis, split_axis=0, concat_axis=0, tiled=True)]
    all_to_all x2 -> x1, waiting for transfers between devices: 33.2 us -> 0.01 us  [across(): return lax.all_to_all(block, axis, split_axis=0, concat_axis=0, tiled=True)]
    pallas_call x1, Pallas kernels: 57.2 us -> 67.4 us  [merged_tokens(): pl.pallas_call(functools.partial(merge_kernel, n_tok), out_shape=(jax.Sha...]
    unnamed x16 -> x31, local copies, waits for them, and re-layouts: 1.27 us -> 9.79 us
    all_gather x2 -> x0, local copies, waits for them, and re-layouts: 7.22 us -> none  [the longest x1 4.11 us: shards(): lax.all_gather(vision_outproj, 'tok', axis=1, tiled=True)]
    all_to_all x2 -> x1, starting transfers between devices: 7.53 us -> 7.28 us  [across(): return lax.all_to_all(block, axis, split_axis=0, concat_axis=0, tiled=True)]
  transfers between devices with their start and end apart: 5 -> 3, of which waited for: 2 -> 0; matrix products, arithmetic and copies ran while one was open for 6% -> 5% of each run, Pallas kernels for 57% -> 68%
where the time goes in v3:
time: 262 us
  Pallas kernels  218 us (83%)
  local copies, waits for them, and re-layouts  21.1 us (8%)
  between operations  13.7 us (5%)
  starting transfers between devices  7.32 us (3%)
    pallas_call x2, Pallas kernels, heads_of(): pl.pallas_call(functools.partial(head_kernel, kind, n_tok), out_shape=jax...  150 us
    pallas_call x1, Pallas kernels, merged_tokens(): pl.pallas_call(functools.partial(merge_kernel, n_tok), out_shape=(jax.Sha...  67.4 us
    unnamed x31, local copies, waits for them, and re-layouts  9.79 us
    all_to_all x1, starting transfers between devices, across(): return lax.all_to_all(block, axis, split_axis=0, concat_axis=0, tiled=True)  7.28 us
  transfers between devices with their start and end apart: 3, of which 0 were waited for; matrix products, arithmetic and copies ran while one was open for 5% of the time, Pallas kernels for 68%

profile of v3, /device:TPU:0, one launch (start us, length us, event | category | flops | bytes accessed | tf_op | source)
XLA Modules:
  0.0 261.6 jit_solution(12304931742410312576)
XLA Ops:
  6.5 1.4 reshape.91
  8.0 0.8 copy.29
  9.2 0.7 copy.30
  10.8 0.6 pad_add_fusion
  11.4 7.3 %all-to-all-start = ((s32[8,1,20]{2,1,0:T(1,128)}), s32[8,1,20]{2,1,0:T(1,128)S(1)}, u32[]{:S(2)}, u32[]{:S(2)}) async-start(s32[8,1,20]{2,1,0:T(1,128)} %bitcast.7), calls=%async_computation | async-start | bytes 8192 | tf_op jit(solution)/shard_map/all_to_all | solution.py:498
  18.7 0.8 constant_dynamic-slice_fusion.x_ref
  19.5 1.2 reshape.89
  20.7 0.9 copy.27
  21.6 0.8 pad.20
  22.4 1.0 reshape.90.weight_ref
  23.3 1.7 reshape.93
  25.0 0.5 copy.28
  25.9 0.5 reshape.94
  27.1 1.0 copy-done.7
  28.0 110.9 %shard_map.100.heads_ref = bf16[8,256,128]{2,1,0:T(8,128)(2,1)S(1)} custom-call(bf16[128,1408]{1,0:T(8,128)(2,1)S(1)} %copy-done.7, bf16[8,176,384]{2,1,0:T(8,128)(2,1)S(1)} %reshape.90.weight_ref, s32[8,4]{1,0:T(8,128)S(1)} %slice.10.info_ref), custom_call_target="tpu_custom_call" | custom-call | flops 2214592512 | bytes 5767168 | tf_op jit(solution)/shard_map/pallas_call | solution.py:458
  139.0 0.8 copy-done.5
  139.8 1.8 copy-done.1
  141.6 1.0 copy-done.6
  142.6 67.4 %shard_map.101 = (bf16[2,64,704]{2,1,0:T(8,128)(2,1)S(1)}, bf16[16,96,384]{2,1,0:T(8,128)(2,1)S(1)}) custom-call(bf16[8,256,128]{2,1,0:T(8,128)(2,1)S(1)} %copy-done.6, bf16[1408,1024]{1,0:T(8,128)(2,1)S(1)} %copy-done.1, bf16[256,1408]{1,0:T(8,128)(2,1)S(1)} %copy-done.2, bf16[704,704]{1,0:T(8,128)(2,1)S(1)} %copy-done.3, ...), custom_call_target="tpu_custom_call" | custom-call | flops 738197504 | bytes 2883584 | tf_op jit(solution)/shard_map/pallas_call | solution.py:692
  210.0 1.0 copy-done.4
  211.5 1.4 slice.11
  213.0 1.8 copy-done
  214.8 39.3 %shard_map.102 = bf16[64,1408]{1,0:T(8,128)(2,1)S(1)} custom-call(bf16[64,1408]{1,0:T(8,128)(2,1)S(1)} %dynamic-slice_select_fusion.x_ref, bf16[1408,384]{1,0:T(8,128)(2,1)S(1)} %bitcast.49, s32[1,2]{1,0:T(1,128)S(1)} %sub.25.info_ref, bf16[1408,1024]{1,0:T(8,128)(2,1)S(1)} %copy-done), custom_call_target="tpu_custom_call" | custom-call | flops 1107296256 | bytes 2883584 | tf_op jit(solution)/shard_map/pallas_call | solution.py:458
  254.1 0.7 copy.32
  (55 shorter events, 2.9 us)
Async XLA Ops:
  6.5 133.2 %all-gather.3.cloned.1.call-start = ((), (), s32[]{:S(2)}) async-start(), calls=%async_computation.1 | async-start | bytes 3244032 | tf_op jit(solution)/shard_map/all_gather | solution.py:759
  6.5 2.4 copy-start.9
  8.0 1.9 copy-start.11
  8.0 2.5 copy-start.12
  8.0 10.7 %copy-start.2 = (bf16[256,1408]{1,0:T(8,128)(2,1)S(1)}, bf16[256,1408]{1,0:T(8,128)(2,1)}, u32[]{:S(2)}) copy-start(bf16[256,1408]{1,0:T(8,128)(2,1)} %patches_ref.1) | copy-start | bytes 2162692
  8.8 10.6 %copy-start.8 = (bf16[176,1,3,704]{3,0,2,1:T(8,128)(2,1)S(1)}, bf16[176,1,3,704]{3,0,2,1:T(8,128)(2,1)}, u32[]{:S(2)}) copy-start(bf16[176,1,3,704]{3,0,2,1:T(8,128)(2,1)} %param.12) | copy-start | bytes 2230276
  8.9 204.1 %all-gather.5.cloned.1.call-start = ((), (), s32[]{:S(2)}) async-start(), calls=%async_computation.2 | async-start | bytes 3063808 | tf_op jit(solution)/shard_map/all_gather | solution.py:760
  11.4 15.3 %all-to-all-start = ((s32[8,1,20]{2,1,0:T(1,128)}), s32[8,1,20]{2,1,0:T(1,128)S(1)}, u32[]{:S(2)}, u32[]{:S(2)}) async-start(s32[8,1,20]{2,1,0:T(1,128)} %bitcast.7), calls=%async_computation | async-start | bytes 8192 | tf_op jit(solution)/shard_map/all_to_all | solution.py:498
  25.8 0.7 copy-start.13
  27.1 1.0 copy-start.7
  28.0 111.7 %copy-start.3 = (bf16[704,704]{1,0:T(8,128)(2,1)S(1)}, bf16[704,704]{1,0:T(8,128)(2,1)}, u32[]{:S(2)}) copy-start(bf16[704,704]{1,0:T(8,128)(2,1)} %merger_ref.1) | copy-start | bytes 2973700
  139.0 0.8 copy-start.5
  139.8 1.8 copy-start.1
  141.6 1.0 copy-start.6
  210.0 1.0 copy-start.4
  211.3 1.6 copy-start.10
  213.0 1.8 copy-start
Sparse Core Ops, SparseCore 0:
  9.5 84.7 all-gather.2
  97.1 82.4 all-gather.4

commit v4 on v3

--- a/solution.py
+++ b/solution.py
@@ -214,7 +214,7 @@
             device_id_type=MESH,
         ).wait_recv()
 
-    def run(act, wait):
+    def run(act, wait, between=lambda: None):
         @pl.when(z < n_z - 1)
         def _():
             act(me, 0)
@@ -248,6 +248,9 @@
 
                     act(me + 2 * k, 2)
                     act(me + 2 * k, 3)
+
+            if k == 2:
+                between()
             if k == 1:
                 wait(side)
                 act(side, 3)
@@ -293,18 +296,21 @@
             for t in others:
                 weight_copy(t, me).start()
 
-    run(lambda t, way: push(t, way).start(), lambda t: arrived(t, core))
-    if kind == "image":
+    def hand_over():
         for t in others:
             @pl.when(mine(t))
             def _():
                 weight_copy(t, t).wait_recv()
                 weight_pass(t).start()
 
+    if kind == "image":
+        run(lambda t, way: push(t, way).start(), lambda t: arrived(t, core), hand_over)
         for t in others:
             @pl.when(jnp.logical_not(mine(t)))
             def _():
                 weight_pass(t).wait_recv()
+    else:
+        run(lambda t, way: push(t, way).start(), lambda t: arrived(t, core))
 
     for t in range(n_tok):
         arrived(t, 1 - core)
@@ -412,8 +418,8 @@
         total = jnp.zeros((half, out_ref.shape[1]), jnp.float32)
         for h in range(n_tok):
             total = total + lax.dot_general(
-                mixed[h, pl.ds(pl.multiple_of(c * half, half), half)],
-                last_weight_ref[:, h * LANES : (h + 1) * LANES],
+                mixed[h, pl.ds(pl.multiple_of(c * half, half), half), 0:HD],
+                last_weight_ref[:, h * HD : (h + 1) * HD],
                 (((1,), (1,)), ((), ())),
                 preferred_element_type=jnp.float32,
             )
@@ -488,12 +494,6 @@
     return split.reshape(head_local, rows, 3 * LANES)
 
 
-def turned(weight, head_local):
-    split = weight.T.reshape(weight.shape[1], head_local, HD)
-    split = jnp.pad(split, ((0, 0), (0, 0), (0, LANES - HD)))
-    return split.reshape(weight.shape[1], head_local * LANES)
-
-
 def across(block, axis):
     return lax.all_to_all(block, axis, split_axis=0, concat_axis=0, tiled=True)
 
@@ -558,8 +558,8 @@
         total = jnp.zeros((half, width), jnp.float32)
         for h in range(n_tok):
             total = total + lax.dot_general(
-                heads_ref[h, pl.ds(pl.multiple_of(c * half, half), half)],
-                out_weight_ref[:, h * LANES : (h + 1) * LANES],
+                heads_ref[h, pl.ds(pl.multiple_of(c * half, half), half), 0:HD],
+                out_weight_ref[:, h * HD : (h + 1) * HD],
                 (((1,), (1,)), ((), ())),
                 preferred_element_type=jnp.float32,
             )
@@ -756,8 +756,8 @@
     vision_blocks = head_columns(vision_inproj, head_local)
     text_depth = decoder_inproj.shape[0]
     text_blocks = jnp.pad(head_columns(decoder_inproj, head_local), ((0, 0), (0, -text_depth % 16), (0, 0)))
-    vision_out = lax.all_gather(turned(vision_outproj, head_local), "tok", axis=0, tiled=True)
-    text_out = lax.all_gather(turned(decoder_outproj, head_local), ("grp", "tok"), axis=0, tiled=True)
+    vision_out = lax.all_gather(vision_outproj.T, "tok", axis=0, tiled=True)
+    text_out = lax.all_gather(decoder_outproj.T, ("grp", "tok"), axis=0, tiled=True)
 
     capacity = patch_count // (2 * n_tok)
     targets = image_positions[0]

time: 262 us -> 239 us (0.912)
  Pallas kernels: 218 us -> 194 us
  local copies, waits for them, and re-layouts: 21.1 us -> 17.5 us
    pallas_call x2, Pallas kernels: 150 us -> 122 us  [heads_of(): pl.pallas_call(functools.partial(head_kernel, kind, n_tok), out_shape=jax...]
    pallas_call x1, Pallas kernels: 67.4 us -> 71.7 us  [merged_tokens(): pl.pallas_call(functools.partial(merge_kernel, n_tok), out_shape=(jax.Sha...]
    unnamed x31 -> x25, local copies, waits for them, and re-layouts: 9.79 us -> 7.88 us
  transfers between devices with their start and end apart: 3 -> 3, of which waited for: 0 -> 0; matrix products, arithmetic and copies ran while one was open for 5% -> 6% of each run, Pallas kernels for 68% -> 66%
where the time goes in v4:
time: 239 us; the launch traced here: 238 us
  Pallas kernels  194 us (81%)
  local copies, waits for them, and re-layouts  17.5 us (7%)
  between operations  13.6 us (6%)
  starting transfers between devices  7.32 us (3%)
  other arithmetic  3.75 us (2%)
    pallas_call x2, Pallas kernels, heads_of(): pl.pallas_call(functools.partial(head_kernel, kind, n_tok), out_shape=jax...  122 us
    pallas_call x1, Pallas kernels, merged_tokens(): pl.pallas_call(functools.partial(merge_kernel, n_tok), out_shape=(jax.Sha...  71.7 us
    unnamed x25, local copies, waits for them, and re-layouts  7.88 us
    all_to_all x1, starting transfers between devices, across(): return lax.all_to_all(block, axis, split_axis=0, concat_axis=0, tiled=True)  7.28 us
  transfers between devices with their start and end apart: 3, of which 0 were waited for; matrix products, arithmetic and copies ran while one was open for 6% of the time, Pallas kernels for 66%

profile of v4, /device:TPU:0, one launch (start us, length us, event | category | flops | bytes accessed | tf_op | source)
XLA Modules:
  0.0 237.7 jit_solution(7269399309411085734)
XLA Ops:
  6.5 0.7 all-gather.3.cloned.1.call-update
  7.3 0.7 all-gather.5.cloned.1.call-update
  8.0 0.7 and_select_fusion.1
  9.0 0.7 fusion.6
  9.9 0.8 reduce-window.7
  10.8 0.6 pad_add_fusion
  11.4 7.3 %all-to-all-start = ((s32[8,1,20]{2,1,0:T(1,128)}), s32[8,1,20]{2,1,0:T(1,128)S(1)}, u32[]{:S(2)}, u32[]{:S(2)}) async-start(s32[8,1,20]{2,1,0:T(1,128)} %bitcast.7), calls=%async_computation | async-start | bytes 8192 | tf_op jit(solution)/shard_map/all_to_all | solution.py:498
  18.7 1.8 constant_dynamic-slice_fusion.x_ref
  20.5 1.2 reshape.77
  21.7 0.9 copy.23
  22.6 0.8 pad.12
  23.4 1.0 reshape.78.weight_ref
  24.4 0.7 reshape.79
  27.1 1.0 copy-done.6
  28.1 85.7 %shard_map.100.heads_ref = bf16[8,256,128]{2,1,0:T(8,128)(2,1)S(1)} custom-call(bf16[128,1408]{1,0:T(8,128)(2,1)S(1)} %copy-done.6, bf16[8,176,384]{2,1,0:T(8,128)(2,1)S(1)} %reshape.78.weight_ref, s32[8,4]{1,0:T(8,128)S(1)} %slice.10.info_ref), custom_call_target="tpu_custom_call" | custom-call | flops 2214592512 | bytes 5767168 | tf_op jit(solution)/shard_map/pallas_call | solution.py:464
  113.8 0.8 copy-done.4
  114.6 1.6 copy-done
  116.2 1.0 copy-done.5
  117.3 71.7 %shard_map.101 = (bf16[2,64,704]{2,1,0:T(8,128)(2,1)S(1)}, bf16[16,96,384]{2,1,0:T(8,128)(2,1)S(1)}) custom-call(bf16[8,256,128]{2,1,0:T(8,128)(2,1)S(1)} %copy-done.5, bf16[1408,704]{1,0:T(8,128)(2,1)S(1)} %copy-done, bf16[256,1408]{1,0:T(8,128)(2,1)S(1)} %copy-done.1, bf16[704,704]{1,0:T(8,128)(2,1)S(1)} %copy-done.2, ...), custom_call_target="tpu_custom_call" | custom-call | flops 738197504 | bytes 2883584 | tf_op jit(solution)/shard_map/pallas_call | solution.py:692
  188.9 1.0 copy-done.3
  190.3 1.4 slice.11
  191.9 1.6 copy-done.7
  193.5 36.7 %shard_map.102 = bf16[64,1408]{1,0:T(8,128)(2,1)S(1)} custom-call(bf16[64,1408]{1,0:T(8,128)(2,1)S(1)} %dynamic-slice_select_fusion.x_ref, bf16[1408,384]{1,0:T(8,128)(2,1)S(1)} %bitcast.41, s32[1,2]{1,0:T(1,128)S(1)} %sub.25.info_ref, bf16[1408,704]{1,0:T(8,128)(2,1)S(1)} %copy-done.7), custom_call_target="tpu_custom_call" | custom-call | flops 1107296256 | bytes 2883584 | tf_op jit(solution)/shard_map/pallas_call | solution.py:464
  230.2 0.7 copy.26
  (45 shorter events, 3.3 us)
Async XLA Ops:
  6.5 14.0 %copy-start.8 = (bf16[176,1,3,704]{3,0,2,1:T(8,128)(2,1)S(1)}, bf16[176,1,3,704]{3,0,2,1:T(8,128)(2,1)}, u32[]{:S(2)}) copy-start(bf16[176,1,3,704]{3,0,2,1:T(8,128)(2,1)} %param.12) | copy-start | bytes 2230276
  6.5 108.1 %all-gather.3.cloned.1.call-start = ((), (), s32[]{:S(2)}) async-start(), calls=%async_computation.1 | async-start | bytes 2433024 | tf_op jit(solution)/shard_map/all_gather | solution.py:759
  7.3 184.6 %all-gather.5.cloned.1.call-start = ((), (), s32[]{:S(2)}) async-start(), calls=%async_computation.2 | async-start | bytes 2297856 | tf_op jit(solution)/shard_map/all_gather | solution.py:760
  11.4 15.3 %all-to-all-start = ((s32[8,1,20]{2,1,0:T(1,128)}), s32[8,1,20]{2,1,0:T(1,128)S(1)}, u32[]{:S(2)}, u32[]{:S(2)}) async-start(s32[8,1,20]{2,1,0:T(1,128)} %bitcast.7), calls=%async_computation | async-start | bytes 8192 | tf_op jit(solution)/shard_map/all_to_all | solution.py:498
  23.4 1.0 copy-start.9
  25.9 0.7 copy-start.11
  27.1 1.0 copy-start.6
  28.1 86.5 %copy-start.1 = (bf16[256,1408]{1,0:T(8,128)(2,1)S(1)}, bf16[256,1408]{1,0:T(8,128)(2,1)}, u32[]{:S(2)}) copy-start(bf16[256,1408]{1,0:T(8,128)(2,1)} %patches_ref.1) | copy-start | bytes 2162692
  28.1 86.5 %copy-start.2 = (bf16[704,704]{1,0:T(8,128)(2,1)S(1)}, bf16[704,704]{1,0:T(8,128)(2,1)}, u32[]{:S(2)}) copy-start(bf16[704,704]{1,0:T(8,128)(2,1)} %merger_ref.1) | copy-start | bytes 2973700
  113.8 0.8 copy-start.4
  114.6 1.6 copy-start
  116.2 1.0 copy-start.5
  188.9 1.0 copy-start.3
  190.1 1.6 copy-start.10
  191.9 1.6 copy-start.7
Sparse Core Ops, SparseCore 0:
  9.5 69.6 all-gather.2
  82.0 75.8 all-gather.4
